TPU v7x, 256 devices: a whole 4x4x8 slice. The times are simulated.
256 devices in a mesh: blk: 8 (over y, x_lo), tr: 32 (over z, x_hi, core).
Axes of the slice: x: 4 (x_hi: 2, x_lo: 2; x = x_hi * 2 + x_lo), y: 4, z: 8, core: 2. Of those that a mesh axis runs over, the one named last changes fastest.
Arguments:
- trial: bfloat16 [8192, 256], P('blk'), may hold values from -6 to 6
- energies: float32 [8192], P(('blk', 'tr')), may hold values from 1 to 3
- kpoint_of: int32 [8192], P('blk'), may hold values from 0 to 15, as said below
- exchange_dens: bfloat16 [8192, 32768], P('blk', 'tr'), may hold values from -0.03125 to 0.03125
- direct_dens: bfloat16 [8192, 4096], P('blk', 'tr'), may hold values from -0.09375 to 0.09375
- coulomb: float32 [32768], P('tr'), may hold values from 0.3 to 3
- screened: bfloat16 [16, 4096, 4096], P('blk', None, 'tr'), may hold values from -0.0234375 to 0.0234375
Outputs:
- applied: float32 [8192, 256], P(('blk', 'tr'))
Inputs may be any that keep to these rules, and one draw needn't show every extreme that they name: `kpoint_of`: transition t has a k-point from (t // 1024) * 2 to (t // 1024) * 2 + 1, and every k-point has a transition.
All inputs are finite; a program needn't handle non-finite values.
Results may differ from a plain program's by a relative error of at most 0.0017.
Values may be sent and summed in bfloat16 or wider, within the bound.
A program may use at most 192 MiB of HBM per device.

v0:
```python
import jax
import jax.numpy as jnp
from jax import lax
from jax.sharding import PartitionSpec as P


def shifted(array, axis, by):
    count = lax.axis_size(axis)
    return lax.ppermute(array, axis, [(i, (i + by) % count) for i in range(count)])


def per_device(trial, energies, kpoint_of, exchange_dens, direct_dens, coulomb, screened):
    group_count = lax.axis_size("blk")
    group_index = lax.axis_index("blk")
    member_index = lax.axis_index("tr")
    vectors = trial.shape[1]
    kpoints = screened.shape[0]
    kpoint_total = kpoints * group_count
    local_ids = kpoint_of - group_index * kpoints
    belongs = local_ids[:, None] == jnp.arange(kpoints, dtype=jnp.int32)[None, :]
    weighted = jnp.where(belongs[:, :, None], trial[:, None, :], jnp.zeros((), trial.dtype))
    own_blocks = jnp.einsum(
        "tg,tan->agn", direct_dens, weighted, preferred_element_type=jnp.float32
    ).astype(jnp.bfloat16)
    all_blocks = lax.all_gather(own_blocks, "blk", axis=0, tiled=True)
    own_kpoints = group_index * kpoints + jnp.arange(kpoints, dtype=jnp.int32)
    empty = jnp.zeros((kpoints, screened.shape[1], vectors), jnp.float32)
    current = screened
    total = empty
    for rotation in range(group_count):
        source_group = (group_index - rotation) % group_count
        block_ids = source_group * kpoints + jnp.arange(current.shape[0], dtype=jnp.int32)
        pick_index = (own_kpoints[:, None] - block_ids[None, :]) % kpoint_total
        picked = all_blocks[pick_index]
        total = total + jnp.einsum(
            "igh,aihn->agn", current, picked, preferred_element_type=jnp.float32
        )
        if rotation + 1 < group_count:
            current = shifted(current, "blk", 1)
    potential = lax.psum_scatter(total.astype(jnp.bfloat16), "tr", scatter_dimension=1, tiled=True)
    direct_all = jnp.einsum(
        "tg,agn->tan", direct_dens, potential, preferred_element_type=jnp.float32
    )
    direct = jnp.sum(jnp.where(belongs[:, :, None], direct_all, jnp.zeros((), jnp.float32)), axis=1)
    projected = jnp.einsum("tg,tn->gn", exchange_dens, trial, preferred_element_type=jnp.float32)
    projected_all = lax.psum(projected, "blk")
    scaled = (coulomb[:, None] * projected_all).astype(jnp.bfloat16)
    exchange_term = jnp.dot(exchange_dens, scaled, preferred_element_type=jnp.float32)
    partial_value = 2.0 * exchange_term - direct
    summed = lax.psum_scatter(partial_value, "tr", scatter_dimension=0, tiled=True)
    row_count = summed.shape[0]
    own_trial = lax.dynamic_slice_in_dim(trial, member_index * row_count, row_count, 0)
    return energies[:, None] * own_trial.astype(jnp.float32) + summed


def solution(mesh):
    in_specs = (
        P("blk", None),
        P(("blk", "tr")),
        P("blk"),
        P("blk", "tr"),
        P("blk", "tr"),
        P("tr"),
        P("blk", None, "tr"),
    )
    out_specs = P(("blk", "tr"), None)
    return jax.shard_map(
        per_device, mesh=mesh, in_specs=in_specs, out_specs=out_specs, check_vma=False
    )
```

profile of v0, /device:TPU:1, one launch (start us, length us, event | category | flops | bytes accessed | tf_op | source)
XLA Modules:
  0.0 731.2 jit_solution(4000284974862805226)
XLA Ops:
  6.5 2.0 collective-permute-start
  8.6 46.0 %collective-permute-done = bf16[2,4096,128]{2,1,0:T(8,128)(2,1)S(1)} collective-permute-done((bf16[2,4096,128]{2,1,0:T(8,128)(2,1)}, bf16[2,4096,128]{2,1,0:T(8,128)(2,1)S(1)}, u32[]{:S(2)}, u32[]{:S(2)}) %collective-permute-start) | collective-permute-done | bytes 2097184 | tf_op jit(solution)/shard_map/ppermute | solution.py:9
  54.6 0.4 collective-permute-start.1
  55.0 45.6 %collective-permute-done.1 = bf16[2,4096,128]{2,1,0:T(8,128)(2,1)S(1)} collective-permute-done((bf16[2,4096,128]{2,1,0:T(8,128)(2,1)S(1)}, bf16[2,4096,128]{2,1,0:T(8,128)(2,1)S(1)}, u32[]{:S(2)}, u32[]{:S(2)}) %collective-permute-start.1) | collective-permute-done | bytes 2097184 | tf_op jit(solution)/shard_map/ppermute | solution.py:9
  100.6 1.4 copy-done.2
  102.2 44.8 %collective-permute-done.2 = bf16[2,4096,128]{2,1,0:T(8,128)(2,1)S(1)} collective-permute-done((bf16[2,4096,128]{2,1,0:T(8,128)(2,1)S(1)}, bf16[2,4096,128]{2,1,0:T(8,128)(2,1)S(1)}, u32[]{:S(2)}, u32[]{:S(2)}) %collective-permute-start.2) | collective-permute-done | bytes 2097184 | tf_op jit(solution)/shard_map/ppermute | solution.py:9
  147.0 0.8 collective-permute-start.3
  147.8 0.5 copy-done.6
  148.3 43.0 %collective-permute-done.3 = bf16[2,4096,128]{2,1,0:T(8,128)(2,1)} collective-permute-done((bf16[2,4096,128]{2,1,0:T(8,128)(2,1)S(1)}, bf16[2,4096,128]{2,1,0:T(8,128)(2,1)}, u32[]{:S(2)}, u32[]{:S(2)}) %collective-permute-start.3) | collective-permute-done | bytes 2097184 | tf_op jit(solution)/shard_map/ppermute | solution.py:9
  191.3 1.1 collective-permute-start.4
  192.4 1.2 copy.15
  193.7 0.7 broadcast_subtract_fusion
  194.4 1.4 fusion.20
  195.8 0.8 copy.16
  196.8 49.6 %collective-permute-done.4 = bf16[2,4096,128]{2,1,0:T(8,128)(2,1)} collective-permute-done((bf16[2,4096,128]{2,1,0:T(8,128)(2,1)}, bf16[2,4096,128]{2,1,0:T(8,128)(2,1)}, u32[]{:S(2)}, u32[]{:S(2)}) %collective-permute-start.4) | collective-permute-done | bytes 2097184 | tf_op jit(solution)/shard_map/ppermute | solution.py:9
  246.3 5.0 collective-permute-start.5
  252.2 8.7 %all-gather.2.cloned.1.call-done = bf16[16,128,256]{2,1,0:T(8,128)(2,1)} async-done(((bf16[2,128,256]{2,1,0:T(8,128)(2,1)}), bf16[16,128,256]{2,1,0:T(8,128)(2,1)}) %all-gather.2.cloned.1.call-update) | async-done | bytes 1048592 | tf_op jit(solution)/shard_map/all_gather | solution.py:25
  261.0 2.6 gather_fusion.6
  263.5 2.5 gather_fusion.5
  266.0 2.5 gather_fusion.4
  268.6 2.5 gather_fusion.3
  271.0 1.3 gather_fusion.2
  272.3 1.3 gather_fusion.1
  273.6 1.3 gather_fusion
  274.9 0.6 gather_fusion.7
  275.5 6.4 fusion.16
  281.9 4.5 fusion.14
  286.4 10.3 %collective-permute-done.5 = bf16[2,4096,128]{2,1,0:T(8,128)(2,1)} collective-permute-done((bf16[2,4096,128]{2,1,0:T(8,128)(2,1)}, bf16[2,4096,128]{2,1,0:T(8,128)(2,1)}, u32[]{:S(2)}, u32[]{:S(2)}) %collective-permute-start.5) | collective-permute-done | bytes 2097184 | tf_op jit(solution)/shard_map/ppermute | solution.py:9
  296.7 0.8 collective-permute-start.6
  297.6 4.6 fusion.12
  302.2 4.6 fusion.10
  306.8 6.2 fusion.8
  313.0 6.2 fusion.6
  319.2 6.2 fusion.4
  325.4 15.4 %collective-permute-done.6 = bf16[2,4096,128]{2,1,0:T(8,128)(2,1)S(1)} collective-permute-done((bf16[2,4096,128]{2,1,0:T(8,128)(2,1)}, bf16[2,4096,128]{2,1,0:T(8,128)(2,1)S(1)}, u32[]{:S(2)}, u32[]{:S(2)}) %collective-permute-start.6) | collective-permute-done | bytes 2097184 | tf_op jit(solution)/shard_map/ppermute | solution.py:9
  340.7 21.2 %fusion.1 = bf16[2,4096,256]{1,2,0:T(8,128)(2,1)} fusion(bf16[2,2,128,256]{3,2,1,0:T(8,128)(2,1)S(1)} %bitcast.138, f32[2,256,4096,1]{2,1,3,0:T(8,128)} %fusion.4, f32[2,256,4096,1]{2,1,3,0:T(8,128)} %fusion.6, f32[2,256,4096,1]{2,1,3,0:T(8,128)} %fusion.8, f32[2,256,4096,1]{2,1,3,0:T(8,128)} %fusion.10, f32[2,256,4096,1]{2,1,3,0:T(8,128)} %fusion.12, ...), kind=kOutput, calls=%fused_computation.16 | convolution fusion | flops 1090519040 | bytes 65273856 | tf_op jit(solution)/shard_map/igh,aihn->agn/dot_general | solution.py:35
  362.0 11.1 %copy.42 = bf16[2,4096,256]{2,0,1:T(2,128)(2,1)} copy(bf16[2,4096,256]{1,2,0:T(8,128)(2,1)} %fusion.1) | data formatting | bytes 8388608
  373.1 4.9 copy.46
  378.1 0.9 copy-done.14
  379.0 1.7 fusion.38
  380.8 137.5 %reduce-scatter.7.cloned.1.call-done = bf16[128,512]{1,0:T(8,128)(2,1)} async-done(((bf16[4096,512]{1,0:T(8,128)(2,1)}), bf16[128,512]{1,0:T(8,128)(2,1)}) %reduce-scatter.7.cloned.1.call-update) | async-done | bytes 131088
  518.3 0.9 reshape.830
  519.2 1.5 fusion.2
  520.7 84.8 %all-reduce.2.cloned.1.call-done = f32[1024,256]{1,0:T(8,128)} async-done(((f32[1024,256]{1,0:T(8,128)}), f32[1024,256]{1,0:T(8,128)}) %all-reduce.2.cloned.1.call-update) | async-done | bytes 1048592 | tf_op jit(solution)/shard_map/psum | solution.py:46
  605.5 2.5 fusion.19
  608.1 1.3 copy.44
  609.4 113.8 %reduce-scatter.9.cloned.1.call-done = f32[32,256]{1,0:T(8,128)} async-done(((f32[1024,256]{1,0:T(8,128)}), f32[32,256]{1,0:T(8,128)}) %reduce-scatter.9.cloned.1.call-update) | async-done | bytes 32784 | tf_op jit(solution)/shard_map/reduce_scatter | solution.py:50
  723.3 1.4 multiply_add_fusion
  (65 shorter events, 1.4 us)
Async XLA Ops:
  6.5 371.5 %copy-start = (bf16[1024,1024]{1,0:T(8,128)(2,1)S(1)}, bf16[1024,1024]{1,0:T(8,128)(2,1)}, u32[]{:S(2)}) copy-start(bf16[1024,1024]{1,0:T(8,128)(2,1)} %param.10) | copy-start | bytes 6291460
  6.5 254.4 %all-gather.2.cloned.1.call-start = ((), (), s32[]{:S(2)}) async-start(), calls=%async_computation.3 | async-start | bytes 1179648 | tf_op jit(solution)/shard_map/all_gather | solution.py:25
  6.5 48.0 %collective-permute-start = (bf16[2,4096,128]{2,1,0:T(8,128)(2,1)}, bf16[2,4096,128]{2,1,0:T(8,128)(2,1)S(1)}, u32[]{:S(2)}, u32[]{:S(2)}) collective-permute-start(bf16[2,4096,128]{2,1,0:T(8,128)(2,1)} %param.13), channel_id=1, source_target_pairs={{0,32},{32,64},{64,96},{96,128},{128,160},{160,192},{192,224},{224... | collective-permute-start | bytes 6291464 | tf_op jit(solution)/shard_map/ppermute | solution.py:9
  54.6 92.4 %copy-start.4 = (bf16[2,4096,128]{2,1,0:T(8,128)(2,1)}, bf16[2,4096,128]{2,1,0:T(8,128)(2,1)S(1)}, u32[]{:S(2)}) copy-start(bf16[2,4096,128]{2,1,0:T(8,128)(2,1)S(1)} %collective-permute-done) | copy-start | bytes 6291460
  54.6 46.0 %collective-permute-start.1 = (bf16[2,4096,128]{2,1,0:T(8,128)(2,1)S(1)}, bf16[2,4096,128]{2,1,0:T(8,128)(2,1)S(1)}, u32[]{:S(2)}, u32[]{:S(2)}) collective-permute-start(bf16[2,4096,128]{2,1,0:T(8,128)(2,1)S(1)} %collective-permute-done), channel_id=1, source_target_pairs={{0,32},{32,64},{64,96},{96,128},{128,160},{160,192},{192,224},{224... | collective-permute-start | bytes 6291464 | tf_op jit(solution)/shard_map/ppermute | solution.py:9
  100.6 1.4 copy-start.2
  101.9 45.1 %collective-permute-start.2 = (bf16[2,4096,128]{2,1,0:T(8,128)(2,1)S(1)}, bf16[2,4096,128]{2,1,0:T(8,128)(2,1)S(1)}, u32[]{:S(2)}, u32[]{:S(2)}) collective-permute-start(bf16[2,4096,128]{2,1,0:T(8,128)(2,1)S(1)} %collective-permute-done.1), channel_id=1, source_target_pairs={{0,32},{32,64},{64,96},{96,128},{128,160},{160,192},{192,224},{224... | collective-permute-start | bytes 6291464 | tf_op jit(solution)/shard_map/ppermute | solution.py:9
  147.0 1.3 copy-start.6
  147.0 44.2 %collective-permute-start.3 = (bf16[2,4096,128]{2,1,0:T(8,128)(2,1)S(1)}, bf16[2,4096,128]{2,1,0:T(8,128)(2,1)}, u32[]{:S(2)}, u32[]{:S(2)}) collective-permute-start(bf16[2,4096,128]{2,1,0:T(8,128)(2,1)S(1)} %collective-permute-done.2), channel_id=1, source_target_pairs={{0,32},{32,64},{64,96},{96,128},{128,160},{160,192},{192,224},{224... | collective-permute-start | bytes 6291464 | tf_op jit(solution)/shard_map/ppermute | solution.py:9
  191.3 55.1 %collective-permute-start.4 = (bf16[2,4096,128]{2,1,0:T(8,128)(2,1)}, bf16[2,4096,128]{2,1,0:T(8,128)(2,1)}, u32[]{:S(2)}, u32[]{:S(2)}) collective-permute-start(bf16[2,4096,128]{2,1,0:T(8,128)(2,1)} %collective-permute-done.3), channel_id=1, source_target_pairs={{0,32},{32,64},{64,96},{96,128},{128,160},{160,192},{192,224},{224... | collective-permute-start | bytes 6291464 | tf_op jit(solution)/shard_map/ppermute | solution.py:9
  196.6 321.7 %reduce-scatter.7.cloned.1.call-start = ((), (), s32[]{:S(2)}) async-start(), calls=%async_computation.4 | async-start | bytes 4325376
  246.3 50.4 %collective-permute-start.5 = (bf16[2,4096,128]{2,1,0:T(8,128)(2,1)}, bf16[2,4096,128]{2,1,0:T(8,128)(2,1)}, u32[]{:S(2)}, u32[]{:S(2)}) collective-permute-start(bf16[2,4096,128]{2,1,0:T(8,128)(2,1)} %collective-permute-done.4), channel_id=1, source_target_pairs={{0,32},{32,64},{64,96},{96,128},{128,160},{160,192},{192,224},{224... | collective-permute-start | bytes 6291464 | tf_op jit(solution)/shard_map/ppermute | solution.py:9
  260.9 10.1 %copy-start.1 = (bf16[16,128,256]{2,1,0:T(8,128)(2,1)S(1)}, bf16[16,128,256]{2,1,0:T(8,128)(2,1)}, u32[]{:S(2)}) copy-start(bf16[16,128,256]{2,1,0:T(8,128)(2,1)} %all-gather.2.cloned.1.call-done) | copy-start | bytes 3145732
  275.4 6.4 copy-start.5
  275.4 6.4 copy-start.13
  281.9 15.7 %copy-start.3 = (bf16[2,4096,128]{2,1,0:T(8,128)(2,1)S(1)}, bf16[2,4096,128]{2,1,0:T(8,128)(2,1)}, u32[]{:S(2)}) copy-start(bf16[2,4096,128]{2,1,0:T(8,128)(2,1)} %copy-done.2) | copy-start | bytes 6291460
  281.9 15.7 %copy-start.12 = (bf16[4,128,256]{2,1,0:T(8,128)(2,1)S(1)}, bf16[4,128,256]{2,1,0:T(8,128)(2,1)}, u32[]{:S(2)}) copy-start(bf16[4,128,256]{2,1,0:T(8,128)(2,1)} %gather_fusion.2) | copy-start | bytes 786436
  296.7 44.0 %collective-permute-start.6 = (bf16[2,4096,128]{2,1,0:T(8,128)(2,1)}, bf16[2,4096,128]{2,1,0:T(8,128)(2,1)S(1)}, u32[]{:S(2)}, u32[]{:S(2)}) collective-permute-start(bf16[2,4096,128]{2,1,0:T(8,128)(2,1)} %collective-permute-done.5), channel_id=1, source_target_pairs={{0,32},{32,64},{64,96},{96,128},{128,160},{160,192},{192,224},{224... | collective-permute-start | bytes 6291464 | tf_op jit(solution)/shard_map/ppermute | solution.py:9
  297.6 4.6 copy-start.7
  297.6 4.6 copy-start.11
  302.2 4.6 copy-start.10
  306.8 6.2 copy-start.9
  313.0 6.2 copy-start.8
  378.0 1.0 copy-start.14
  378.0 141.2 %copy-start.17 = (bf16[1024,128]{1,0:T(8,128)(2,1)S(1)}, bf16[1024,128]{1,0:T(8,128)(2,1)}, u32[]{:S(2)}) copy-start(bf16[1024,128]{1,0:T(8,128)(2,1)} %param.11) | copy-start | bytes 786436
  378.0 227.5 %all-reduce.2.cloned.1.call-start = ((), (), s32[]{:S(2)}) async-start(), calls=%async_computation.2 | async-start | bytes 2097152 | tf_op jit(solution)/shard_map/psum | solution.py:46
  380.7 224.8 %copy-start.15 = (f32[1024]{0:T(1024)S(1)}, f32[1024]{0:T(1024)}, u32[]{:S(2)}) copy-start(f32[1024]{0:T(1024)} %param.12) | copy-start | bytes 12292
  380.8 342.5 %reduce-scatter.9.cloned.1.call-start = ((), (), s32[]{:S(2)}) async-start(), calls=%async_computation.5 | async-start | bytes 1081344 | tf_op jit(solution)/shard_map/reduce_scatter | solution.py:50
  608.0 115.2 %copy-start.16 = (f32[32]{0:T(128)S(1)}, f32[32]{0:T(128)}, u32[]{:S(2)}) copy-start(f32[32]{0:T(128)} %param.8) | copy-start | bytes 388
Sparse Core Ops, SparseCore 0:
  196.7 64.2 all-gather.1
  378.1 140.0 reduce-scatter.6
  521.1 84.3 all-reduce.1
  610.0 113.2 reduce-scatter.8
where the time goes:
time: 736 us; the launch traced here: 731 us
  waiting for transfers between devices  599 us (81%)
  matrix products  67 us (9%)
  local copies, waits for them, and re-layouts  38.3 us (5%)
  between operations  13.5 us (2%)
  starting transfers between devices  10.6 us (1%)
    ppermute x7, waiting for transfers between devices, shifted(): lax.ppermute(array, axis, [(i, (i + by) % count) for i in range(count)])  255 us
    unnamed x5, waiting for transfers between devices  138 us
    reduce_scatter x1, waiting for transfers between devices, per_device(): lax.psum_scatter(partial_value, 'tr', scatter_dimension=0, tiled=True)  114 us
    psum x1, waiting for transfers between devices, per_device(): projected_all = lax.psum(projected, 'blk')  84.8 us
    dot_general x8, matrix products, per_device(): jnp.einsum('igh,aihn->agn', current, picked, preferred_element_type=jnp.f...  59.9 us
    unnamed x41, local copies, waits for them, and re-layouts  22.4 us
  transfers between devices with their start and end apart: 11, of which 11 were waited for; matrix products, arithmetic and copies ran while one was open for 9% of the time, Pallas kernels for 0%

commit v1 on v0

v1 whole, which is shorter than its diff:
```python
import math

import jax
import jax.numpy as jnp
from jax import lax
from jax.sharding import PartitionSpec as P


def turn(value, angle):
    re, im = value
    c, s = math.cos(angle), math.sin(angle)
    if abs(s) < 1e-9:
        return value
    if abs(c) < 1e-9:
        return (None if im is None else -s * im), s * re
    if im is None:
        return c * re, s * re
    return c * re - s * im, s * re + c * im


def plus(a, b):
    return b if a is None else a if b is None else a + b


def minus(a, b):
    return a if b is None else -b if a is None else a - b


def forward(x):
    n = len(x)
    if n == 1:
        return [(x[0], None)]
    if n == 2:
        return [(x[0] + x[1], None), (x[0] - x[1], None)]
    even, odd = forward(x[0::2]), forward(x[1::2])
    out = [None] * (n // 2 + 1)
    for w in range(n // 4 + 1):
        e, o = even[w], turn(odd[w], -2 * math.pi * w / n)
        out[w] = plus(e[0], o[0]), plus(e[1], o[1])
        if w != n // 2 - w:
            re, im = minus(e[0], o[0]), minus(e[1], o[1])
            out[n // 2 - w] = re, None if im is None else -im
    return out


def backward(y):
    n = 2 * (len(y) - 1)
    if n == 2:
        return [y[0][0] + y[1][0], y[0][0] - y[1][0]]
    even, odd = [], []
    for w in range(n // 4 + 1):
        a, b = y[w], y[n // 2 - w]
        even.append((plus(a[0], b[0]), minus(a[1], b[1])))
        odd.append(turn((minus(a[0], b[0]), plus(a[1], b[1])), 2 * math.pi * w / n))
    for part in (even, odd):
        part[0], part[-1] = (part[0][0], None), (part[-1][0], None)
    out = [None] * n
    out[0::2], out[1::2] = backward(even), backward(odd)
    return out


def per_device(trial, energies, kpoint_of, exchange_dens, direct_dens, coulomb, screened):
    groups, members = lax.axis_size("blk"), lax.axis_size("tr")
    group, member = lax.axis_index("blk"), lax.axis_index("tr")
    kpoints, waves, own_waves = screened.shape
    vectors = trial.shape[1]
    rows = waves // groups // members
    total_k = kpoints * groups
    half = total_k // 2
    f32, bf16 = jnp.float32, jnp.bfloat16

    local = kpoint_of - group * kpoints
    belongs = local[:, None] == jnp.arange(kpoints, dtype=jnp.int32)[None, :]
    masked = jnp.where(belongs[:, :, None], direct_dens[:, None, :], jnp.zeros((), bf16))
    masked = masked.reshape(masked.shape[0], kpoints * own_waves)
    own_blocks = jnp.einsum("tg,tn->gn", masked, trial, preferred_element_type=f32).astype(bf16)
    blocks = lax.all_gather(own_blocks.reshape(kpoints, own_waves, vectors), "blk", axis=0, tiled=True)

    s = screened.reshape(kpoints, members, groups, rows, own_waves)
    s = lax.all_to_all(s, "blk", split_axis=2, concat_axis=0, tiled=True)
    s = s.reshape(total_k, members * rows, own_waves)

    sh = forward([s[q].astype(f32) for q in range(total_k)])
    bh = forward([blocks[q].astype(f32) for q in range(total_k)])
    zero = jnp.zeros((own_waves, vectors), bf16)
    lhs, rhs = [], []
    for w in range(half):
        a, b = (sh[0][0], sh[half][0]) if w == 0 else sh[w]
        c, d = (bh[0][0], bh[half][0]) if w == 0 else bh[w]
        c, d = c.astype(bf16), d.astype(bf16)
        lhs.append(jnp.concatenate([a.astype(bf16), b.astype(bf16)], axis=1))
        rows_of = [[c, zero], [zero, d]] if w == 0 else [[c, d], [-d, c]]
        rhs.append(jnp.concatenate([jnp.concatenate(r, axis=1) for r in rows_of], axis=0))
    out = jnp.einsum("fgh,fhn->fgn", jnp.stack(lhs), jnp.stack(rhs), preferred_element_type=f32)
    out = out.astype(bf16).reshape(half, members, rows, 2 * vectors)
    out = lax.psum_scatter(out, "tr", scatter_dimension=1, tiled=True)[:, 0].astype(f32)
    parts = [(out[w, :, :vectors], out[w, :, vectors:]) for w in range(half)]
    freq = [(parts[0][0], None)] + parts[1:] + [(parts[0][1], None)]
    total = jnp.stack(backward(freq)) * (1.0 / total_k)
    potential = lax.all_to_all(total.astype(bf16), "blk", split_axis=0, concat_axis=1, tiled=True)

    direct = jnp.dot(masked, potential.reshape(kpoints * own_waves, vectors), preferred_element_type=f32)

    projected = jnp.einsum("tg,tn->gn", exchange_dens, trial, preferred_element_type=f32)
    projected = lax.psum_scatter(projected, "blk", scatter_dimension=0, tiled=True)
    part = projected.shape[0]
    own_coulomb = lax.dynamic_slice_in_dim(coulomb, group * part, part, 0)
    scaled = lax.all_gather((own_coulomb[:, None] * projected).astype(bf16), "blk", axis=0, tiled=True)
    exchange_term = jnp.dot(exchange_dens, scaled, preferred_element_type=f32)

    summed = lax.psum_scatter(2.0 * exchange_term - direct, "tr", scatter_dimension=0, tiled=True)
    row_count = summed.shape[0]
    own_trial = lax.dynamic_slice_in_dim(trial, member * row_count, row_count, 0)
    return energies[:, None] * own_trial.astype(f32) + summed


def solution(mesh):
    in_specs = (
        P("blk", None),
        P(("blk", "tr")),
        P("blk"),
        P("blk", "tr"),
        P("blk", "tr"),
        P("tr"),
        P("blk", None, "tr"),
    )
    out_specs = P(("blk", "tr"), None)
    return jax.shard_map(
        per_device, mesh=mesh, in_specs=in_specs, out_specs=out_specs, check_vma=False
    )
```

time: 736 us -> 389 us (0.53)
  waiting for transfers between devices: 599 us -> 279 us
  matrix products: 67 us -> 9.22 us
  other arithmetic: 2.32 us -> 33.9 us
  local copies, waits for them, and re-layouts: 38.3 us -> 11.4 us
  blocking collectives: 0 us -> 26.4 us
    ppermute x7 -> x0, waiting for transfers between devices: 255 us -> none  [shifted(): lax.ppermute(array, axis, [(i, (i + by) % count) for i in range(count)])]
    unnamed x5 -> x4, waiting for transfers between devices: 138 us -> 0.07 us
    reduce_scatter x1 -> x3, waiting for transfers between devices: 114 us -> 236 us  [the longest x1 113 us: per_device(): lax.psum_scatter(2.0 * exchange_term - direct, 'tr', scatter_dimension=0,...]
    psum x1 -> x0, waiting for transfers between devices: 84.8 us -> none  [per_device(): projected_all = lax.psum(projected, 'blk')]
    dot_general x12 -> x5, matrix products: 67 us -> 9.22 us  [the longest x1 2.37 us: per_device(): jnp.dot(masked, potential.reshape(kpoints * own_waves, vectors), preferre...]
    all_to_all x0 -> x2, waiting for transfers between devices: none -> 42.7 us  [the longest x1 39 us: per_device(): s = lax.all_to_all(s, 'blk', split_axis=2, concat_axis=0, tiled=True)]
    all_gather x0 -> x1, blocking collectives: none -> 26.4 us  [per_device(): lax.all_gather((own_coulomb[:, None] * projected).astype(bf16), 'blk', ax...]
    convert_element_type x0 -> x16, other arithmetic: none -> 21.7 us  [the longest x8 16 us: per_device(): lhs.append(jnp.concatenate([a.astype(bf16), b.astype(bf16)], axis=1))]
  transfers between devices with their start and end apart: 11 -> 6, of which waited for: 11 -> 5; matrix products, arithmetic and copies ran while one was open for 9% -> 9% of each run, Pallas kernels for 0% -> 0%
where the time goes in v1:
time: 389 us; the launch traced here: 383 us
  waiting for transfers between devices  279 us (72%)
  other arithmetic  33.9 us (9%)
  blocking collectives  26.4 us (7%)
  between operations  13.6 us (3%)
  local copies, waits for them, and re-layouts  11.4 us (3%)
  starting transfers between devices  10.3 us (3%)
  matrix products  9.22 us (2%)
    reduce_scatter x1, waiting for transfers between devices, per_device(): lax.psum_scatter(2.0 * exchange_term - direct, 'tr', scatter_dimension=0,...  113 us
    reduce_scatter x1, waiting for transfers between devices, per_device(): lax.psum_scatter(out, 'tr', scatter_dimension=1, tiled=True)[:, 0]  104 us
    all_to_all x1, waiting for transfers between devices, per_device(): s = lax.all_to_all(s, 'blk', split_axis=2, concat_axis=0, tiled=True)  39 us
    all_gather x1, blocking collectives, per_device(): lax.all_gather((own_coulomb[:, None] * projected).astype(bf16), 'blk', ax...  26.4 us
    reduce_scatter x1, waiting for transfers between devices, per_device(): lax.psum_scatter(projected, 'blk', scatter_dimension=0, tiled=True)  19 us
    convert_element_type x8, other arithmetic, per_device(): lhs.append(jnp.concatenate([a.astype(bf16), b.astype(bf16)], axis=1))  16 us
  transfers between devices with their start and end apart: 6, of which 5 were waited for; matrix products, arithmetic and copies ran while one was open for 9% of the time, Pallas kernels for 0%

profile of v1, /device:TPU:1, one launch (start us, length us, event | category | flops | bytes accessed | tf_op | source)
XLA Modules:
  0.0 383.4 jit_solution(7784519163078785653)
XLA Ops:
  6.5 0.8 broadcast_subtract_fusion
  7.4 0.2 iota_compare_fusion.2
  7.6 5.8 %broadcast_select_fusion = bf16[1024,2,128]{2,1,0:T(2,128)(2,1)S(1)} fusion(pred[1024,2]{1,0:T(8,128)(4,1)S(1)} %iota_compare_fusion.2, bf16[1024,128]{1,0:T(8,128)(2,1)} %param.11), kind=kLoop, calls=%fused_computation.5 | loop fusion | flops 262144 | bytes 788480 | tf_op jit(solution)/shard_map/jit(_where)/select_n | solution.py:74
  13.5 0.8 copy-done.2
  14.3 2.1 convolution_convert_fusion.1
  16.3 3.5 copy.28
  19.8 6.1 %all-to-all-start = ((bf16[2,32,8,16,128]{4,3,1,0,2:T(8,128)(2,1)}), bf16[2,32,8,16,128]{4,3,1,0,2:T(8,128)(2,1)}, u32[]{:S(2)}, u32[]{:S(2)}) async-start(bf16[2,32,8,16,128]{4,3,1,0,2:T(8,128)(2,1)} %copy.28), calls=%async_computation.1 | async-start | bytes 4194304 | tf_op jit(solution)/shard_map/all_to_all | solution.py:80
  25.9 0.0 reduce-scatter.6.cloned.1.call-start
  26.0 1.8 fusion.114
  27.7 0.0 reduce-scatter.8.cloned.1.call-start
  27.8 39.0 %all-to-all-done = bf16[2,32,8,16,128]{4,3,1,0,2:T(8,128)(2,1)} async-done(((bf16[2,32,8,16,128]{4,3,1,0,2:T(8,128)(2,1)}), bf16[2,32,8,16,128]{4,3,1,0,2:T(8,128)(2,1)}, u32[]{:S(2)}, u32[]{:S(2)}) %all-to-all-start) | async-done | bytes 2097184 | tf_op jit(solution)/shard_map/all_to_all | solution.py:80
  66.8 2.5 fusion.44
  69.3 2.5 fusion.43
  71.9 2.6 fusion.42
  74.5 1.8 fusion.52
  76.3 2.5 fusion.55
  78.9 2.0 fusion.57
  80.9 1.4 fusion.73
  82.3 1.4 fusion.72
  83.7 1.1 fusion.54
  84.8 1.8 fusion.53
  86.6 1.6 fusion.49
  88.6 0.9 copy-done.1
  89.5 0.1 fusion.98
  89.7 0.2 fusion.96
  89.8 0.1 fusion.81
  90.0 0.1 fusion.84
  90.1 0.4 copy-done.8
  90.6 0.2 fusion.102
  90.8 0.1 fusion.104
  90.9 0.1 fusion.77
  91.2 1.3 convolution_convert_fusion
  92.4 2.4 copy.29
  94.9 0.8 dynamic_slice.7
  95.7 19.0 %reduce-scatter.6.cloned.1.call-done = f32[128,256]{1,0:T(8,128)} async-done(((f32[1024,256]{1,0:T(8,128)}), f32[128,256]{1,0:T(8,128)}) %reduce-scatter.6.cloned.1.call-update) | async-done | bytes 131088 | tf_op jit(solution)/shard_map/reduce_scatter | solution.py:105
  114.7 1.0 multiply_convert_fusion.3
  115.7 26.4 %all_gather.6 = bf16[1024,256]{1,0:T(8,128)(2,1)} all-gather(bf16[128,256]{1,0:T(8,128)(2,1)S(1)} %multiply_convert_fusion.3), channel_id=1, replica_groups=mesh['blk'=8,'tr'=32] {'blk'}, dimensions={0}, use_global_device_ids=true | all-gather | bytes 589824 | tf_op jit(solution)/shard_map/all_gather | solution.py:108
  142.2 103.7 %reduce-scatter.8.cloned.1.call-done = bf16[8,1,16,512]{3,2,0,1:T(8,128)(2,1)} async-done(((bf16[8,32,16,512]{3,2,0,1:T(8,128)(2,1)}), bf16[8,1,16,512]{3,2,0,1:T(8,128)(2,1)}) %reduce-scatter.8.cloned.1.call-update) | async-done | bytes 131088 | tf_op jit(solution)/shard_map/reduce_scatter | solution.py:96
  245.9 0.9 bitcast_convert_fusion
  247.2 0.7 multiply_convert_fusion.1
  247.9 4.1 %all-to-all-start.1 = ((bf16[16,16,256]{2,1,0:T(8,128)(2,1)}), bf16[16,16,256]{2,1,0:T(8,128)(2,1)S(1)}, u32[]{:S(2)}, u32[]{:S(2)}) async-start(bf16[16,16,256]{2,1,0:T(8,128)(2,1)} %multiply_convert_fusion.1), calls=%async_computation.3 | async-start | bytes 262144 | tf_op jit(solution)/shard_map/all_to_all | solution.py:100
  251.9 0.0 reduce-scatter.10.cloned.1.call-start
  252.0 1.8 fusion
  253.8 3.7 all-to-all-done.1
  257.5 2.4 convolution_subtract_fusion
  259.8 2.5 copy.34
  262.4 113.0 %reduce-scatter.10.cloned.1.call-done = f32[32,256]{1,0:T(8,128)} async-done(((f32[1024,256]{1,0:T(8,128)}), f32[32,256]{1,0:T(8,128)}) %reduce-scatter.10.cloned.1.call-update) | async-done | bytes 32784 | tf_op jit(solution)/shard_map/reduce_scatter | solution.py:111
  375.4 1.4 multiply_add_fusion.4
  (62 shorter events, 0.8 us)
Async XLA Ops:
  6.5 19.4 %copy-start = (bf16[1024,1024]{1,0:T(8,128)(2,1)S(1)}, bf16[1024,1024]{1,0:T(8,128)(2,1)}, u32[]{:S(2)}) copy-start(bf16[1024,1024]{1,0:T(8,128)(2,1)} %param.10) | copy-start | bytes 6291460
  6.5 74.4 %all-gather.2.cloned.1.call-start = ((), (), s32[]{:S(2)}) async-start(), calls=%async_computation.6 | async-start | bytes 1179648 | tf_op jit(solution)/shard_map/all_gather | solution.py:77
  13.4 0.8 copy-start.2
  19.8 6.1 %copy-start.11 = (bf16[1024,256]{1,0:T(8,128)(2,1)S(1)}, bf16[1024,256]{1,0:T(8,128)(2,1)}, u32[]{:S(2)}) copy-start(bf16[1024,256]{1,0:T(8,128)(2,1)} %param.7) | copy-start | bytes 1572868
  19.8 47.0 %all-to-all-start = ((bf16[2,32,8,16,128]{4,3,1,0,2:T(8,128)(2,1)}), bf16[2,32,8,16,128]{4,3,1,0,2:T(8,128)(2,1)}, u32[]{:S(2)}, u32[]{:S(2)}) async-start(bf16[2,32,8,16,128]{4,3,1,0,2:T(8,128)(2,1)} %copy.28), calls=%async_computation.1 | async-start | bytes 4194304 | tf_op jit(solution)/shard_map/all_to_all | solution.py:80
  25.9 88.8 %reduce-scatter.6.cloned.1.call-start = ((), (), s32[]{:S(2)}) async-start(), calls=%async_computation.5 | async-start | bytes 1179648 | tf_op jit(solution)/shard_map/reduce_scatter | solution.py:105
  27.7 218.2 %reduce-scatter.8.cloned.1.call-start = ((), (), s32[]{:S(2)}) async-start(), calls=%async_computation.7 | async-start | bytes 4325376 | tf_op jit(solution)/shard_map/reduce_scatter | solution.py:96
  80.9 2.8 copy-start.3
  84.8 3.5 copy-start.6
  84.8 3.5 copy-start.7
  86.6 1.9 copy-start.4
  86.6 1.9 copy-start.5
  86.6 1.9 copy-start.9
  86.6 1.9 copy-start.10
  88.3 1.2 copy-start.1
  89.6 0.9 copy-start.8
  247.9 9.6 %all-to-all-start.1 = ((bf16[16,16,256]{2,1,0:T(8,128)(2,1)}), bf16[16,16,256]{2,1,0:T(8,128)(2,1)S(1)}, u32[]{:S(2)}, u32[]{:S(2)}) async-start(bf16[16,16,256]{2,1,0:T(8,128)(2,1)} %multiply_convert_fusion.1), calls=%async_computation.3 | async-start | bytes 262144 | tf_op jit(solution)/shard_map/all_to_all | solution.py:100
  251.9 123.5 %reduce-scatter.10.cloned.1.call-start = ((), (), s32[]{:S(2)}) async-start(), calls=%async_computation.8 | async-start | bytes 1081344 | tf_op jit(solution)/shard_map/reduce_scatter | solution.py:111
  259.8 115.6 %copy-start.12 = (f32[32]{0:T(128)S(1)}, f32[32]{0:T(128)}, u32[]{:S(2)}) copy-start(f32[32]{0:T(128)} %param.8) | copy-start | bytes 388
Sparse Core Ops, SparseCore 0:
  16.5 56.6 all-gather.1
  75.6 39.0 reduce-scatter.5
  119.0 126.8 reduce-scatter.7
  262.5 112.8 reduce-scatter.9

commit v2 on v1

v2 whole, which is shorter than its diff:
```python
import functools
import math

import jax
import jax.numpy as jnp
from jax import lax
from jax.experimental import pallas as pl
from jax.experimental.pallas import tpu as pltpu
from jax.sharding import PartitionSpec as P

F32, BF16 = jnp.float32, jnp.bfloat16
NT_DIMS = (((1,), (1,)), ((), ()))


def turn(value, angle):
    re, im = value
    c, s = math.cos(angle), math.sin(angle)
    if abs(s) < 1e-9:
        return value
    if abs(c) < 1e-9:
        return (None if im is None else -s * im), s * re
    if im is None:
        return c * re, s * re
    return c * re - s * im, s * re + c * im


def plus(a, b):
    return b if a is None else a if b is None else a + b


def minus(a, b):
    return a if b is None else -b if a is None else a - b


def forward(x):
    n = len(x)
    if n == 2:
        return [(x[0] + x[1], None), (x[0] - x[1], None)]
    even, odd = forward(x[0::2]), forward(x[1::2])
    out = [None] * (n // 2 + 1)
    for w in range(n // 4 + 1):
        e, o = even[w], turn(odd[w], -2 * math.pi * w / n)
        out[w] = plus(e[0], o[0]), plus(e[1], o[1])
        if w != n // 2 - w:
            re, im = minus(e[0], o[0]), minus(e[1], o[1])
            out[n // 2 - w] = re, None if im is None else -im
    return out


def backward(y):
    n = 2 * (len(y) - 1)
    if n == 2:
        return [y[0][0] + y[1][0], y[0][0] - y[1][0]]
    even, odd = [], []
    for w in range(n // 4 + 1):
        a, b = y[w], y[n // 2 - w]
        even.append((plus(a[0], b[0]), minus(a[1], b[1])))
        odd.append(turn((minus(a[0], b[0]), plus(a[1], b[1])), 2 * math.pi * w / n))
    for part in (even, odd):
        part[0], part[-1] = (part[0][0], None), (part[-1][0], None)
    out = [None] * n
    out[0::2], out[1::2] = backward(even), backward(odd)
    return out


def wait_bytes(ref, sem):
    pltpu.make_async_copy(ref, ref, sem).wait()


def send(src, dst, send_sem, recv_sem, device):
    pltpu.make_async_remote_copy(
        src_ref=src, dst_ref=dst, send_sem=send_sem, recv_sem=recv_sem,
        device_id=device, device_id_type=pl.DeviceIdType.MESH,
    ).start()


def kernel(
    sizes, s_hbm, e_hbm, d_hbm, t_hbm, kp, coul, out,
    e, d, t, tt, d2, s_in, b_out, b_in, rhs, lhs, part, core_in, ring_out, ring_in,
    proj, proj_in, scaled, eterm, p_out, p_in, prhs, f_part, f_core, t_out, t_in,
    sem_load, sem_s_out, sem_s_in, sem_b, sem_x, sem_c_out, sem_c_in, sem_r_out, sem_r_in,
    sem_p, sem_f_out, sem_f_in, sem_t,
):
    groups, zs, kpts, rows, waves, vecs, parts = sizes
    total_k = groups * kpts
    half = total_k // 2
    step = half // parts
    gb = lax.axis_index("blk")
    me = lax.axis_index("tr")
    z, xh, c = me // 4, (me // 2) % 2, me % 2

    def place(zz, xx, cc):
        return zz * 4 + xx * 2 + cc

    other = {"tr": place(z, xh, 1 - c)}
    onward = {"tr": place((z + 1 - 2 * c + zs) % zs, xh, c)}

    loads = [pltpu.make_async_copy(a, b, sem_load.at[i]) for i, (a, b) in enumerate(((t_hbm, t), (d_hbm, d), (e_hbm, e)))]
    for load in loads:
        load.start()

    barrier = pltpu.get_barrier_semaphore()

    def greet(device):
        pl.semaphore_signal(barrier, inc=1, device_id=device, device_id_type=pl.DeviceIdType.MESH)

    greet(other)

    def greet_blk(i, carry):
        greet({"blk": (gb + i // 2) % groups, "tr": place(z, (xh + i) % 2, c)})
        return carry

    def greet_tr(i, carry):
        greet({"tr": place((z + i // 2) % zs, (xh + i) % 2, c)})
        return carry

    lax.fori_loop(1, 2 * groups, greet_blk, 0)
    lax.fori_loop(1, 2 * zs, greet_tr, 0)

    ring_in[0] = jnp.zeros(ring_in.shape[1:], BF16)
    loads[0].wait()
    count = t.shape[0]
    unit = min(128, count)
    tt[...] = t[...].T
    loads[1].wait()
    eye = lax.broadcasted_iota(jnp.int32, (unit, unit), 0) == lax.broadcasted_iota(jnp.int32, (unit, unit), 1)
    for i in range(count // unit):
        local = (kp[:, i * unit : (i + 1) * unit] - gb * kpts).astype(F32)
        column = jnp.sum(jnp.where(eye, jnp.broadcast_to(local, (unit, unit)), 0.0), axis=1, keepdims=True)
        dens = d[i * unit : (i + 1) * unit, :].astype(F32)
        for k in range(kpts):
            mask = jnp.where(column == float(k), 1.0, 0.0)
            d2[i * unit : (i + 1) * unit, k * waves : (k + 1) * waves] = (dens * mask).astype(BF16)
    own = jnp.dot(tt[...], d2[...], preferred_element_type=F32)
    for k in range(kpts):
        b_out[k] = own[:, k * waves : (k + 1) * waves].astype(BF16)

    pl.semaphore_wait(barrier, 2 * groups + 2 * zs - 1)

    def send_s(stage, carry):
        for ab, zz in enumerate(((z - 1 - stage + 2 * zs) % zs, (z + 1 + stage) % zs)):
            pltpu.make_async_copy(s_hbm.at[:, zz, :, ab, gb], s_in.at[stage, gb, ab], sem_s_in.at[stage]).start()

        def to_peer(i, inner):
            peer = (gb + i) % groups
            for ab, zz in enumerate(((z - 1 - stage + 2 * zs) % zs, (z + 1 + stage) % zs)):
                send(s_hbm.at[:, zz, :, ab, peer], s_in.at[stage, gb, ab], sem_s_out.at[stage], sem_s_in.at[stage], {"blk": peer})
            return inner

        return lax.fori_loop(1, groups, to_peer, carry)

    send_s(0, 0)
    pltpu.make_async_copy(b_out, b_in.at[gb], sem_b.at[1]).start()

    def send_b(i, carry):
        send(b_out, b_in.at[gb], sem_b.at[0], sem_b.at[1], {"blk": (gb + i) % groups})
        return carry

    lax.fori_loop(1, groups, send_b, 0)
    send_s(1, 0)

    loads[2].wait()
    own_waves = e.shape[1]
    share = own_waves // groups
    chunk = min(256, own_waves)
    for i in range(own_waves // chunk):
        cols = slice(i * chunk, (i + 1) * chunk)
        proj[:, cols] = jnp.dot(tt[...], e[:, cols], preferred_element_type=F32).astype(BF16)

    def cut(index):
        return pl.ds(pl.multiple_of(index * share, share), share)

    pltpu.make_async_copy(proj.at[:, cut(gb)], proj_in.at[gb], sem_x.at[1]).start()

    def send_proj(i, carry):
        peer = (gb + i) % groups
        send(proj.at[:, cut(peer)], proj_in.at[gb], sem_x.at[0], sem_x.at[1], {"blk": peer})
        return carry

    lax.fori_loop(1, groups, send_proj, 0)
    lax.fori_loop(2, zs, send_s, 0)

    wait_bytes(b_in, sem_b.at[1])
    tile = min(16, vecs)

    def transform_b(i, carry):
        at = pl.ds(pl.multiple_of(i * tile, tile), tile)
        low = pl.ds(pl.multiple_of(vecs + i * tile, tile), tile)
        freq = forward([b_in[q // kpts, q % kpts, at, :].astype(F32) for q in range(total_k)])
        zero = jnp.zeros((tile, waves), BF16)
        for f in range(half):
            re, im = (freq[0][0], freq[half][0]) if f == 0 else freq[f]
            re, im = re.astype(BF16), im.astype(BF16)
            rhs[f, at, 0:waves] = re
            rhs[f, at, waves:] = zero if f == 0 else -im
            rhs[f, low, 0:waves] = zero if f == 0 else im
            rhs[f, low, waves:] = im if f == 0 else re
        return carry

    lax.fori_loop(0, vecs // tile, transform_b, 0)

    def multiply(stage):
        wait_bytes(s_in.at[stage], sem_s_in.at[stage])
        for ab in range(2):
            for xx in range(2):
                freq = forward([s_in[stage, q // kpts, ab, q % kpts, xx].astype(F32) for q in range(total_k)])
                at = slice((ab * 2 + xx) * rows, (ab * 2 + xx + 1) * rows)
                for f in range(half):
                    re, im = (freq[0][0], freq[half][0]) if f == 0 else freq[f]
                    lhs[f, at, 0:waves] = re.astype(BF16)
                    lhs[f, at, waves:] = im.astype(BF16)
        for p in range(parts):
            for f in range(p * step, (p + 1) * step):
                value = lax.dot_general(lhs[f], rhs[f], NT_DIMS, preferred_element_type=F32)
                part[stage, 0, f] = value[: 2 * rows].astype(BF16)
                part[stage, 1, f] = value[2 * rows :].astype(BF16)
            cut_f = pl.ds(p * step, step)
            send(part.at[stage, 1 - c, cut_f], core_in.at[stage, cut_f], sem_c_out.at[stage], sem_c_in.at[stage, p], other)

    def pass_on(stage):
        for p in range(parts):
            cut_f = pl.ds(p * step, step)
            wait_bytes(core_in.at[stage, cut_f], sem_c_in.at[stage, p])

            @pl.when(stage > 0)
            def _():
                wait_bytes(ring_in.at[stage, cut_f], sem_r_in.at[stage, p])

            for f in range(p * step, (p + 1) * step):
                value = part[stage, c, f].astype(F32) + core_in[stage, f].astype(F32) + ring_in[stage, f].astype(F32)
                ring_out[stage, f] = value.astype(BF16)

            @pl.when(stage < zs - 1)
            def _():
                send(ring_out.at[stage, cut_f], ring_in.at[stage + 1, cut_f], sem_r_out.at[stage], sem_r_in.at[stage + 1, p], onward)

    def reduce_projection():
        wait_bytes(proj_in, sem_x.at[1])
        total = proj_in[0].astype(F32)
        for i in range(1, groups):
            total = total + proj_in[i].astype(F32)
        scaled[:, cut(gb)] = (coul[pl.ds(gb, 1), :] * total).astype(BF16)

        def send_scaled(i, carry):
            send(scaled.at[:, cut(gb)], scaled.at[:, cut(gb)], sem_x.at[2], sem_x.at[3], {"blk": (gb + i) % groups})
            return carry

        lax.fori_loop(1, groups, send_scaled, 0)

    def exchange():
        wait_bytes(scaled.at[:, pl.ds(0, (groups - 1) * share)], sem_x.at[3])
        chunk_t = min(256, count)

        def do(i, carry):
            at = pl.ds(pl.multiple_of(i * chunk_t, chunk_t), chunk_t)
            eterm[at, :] = 2.0 * lax.dot_general(e[at, :], scaled[...], NT_DIMS, preferred_element_type=F32)
            return carry

        lax.fori_loop(0, count // chunk_t, do, 0)

    def stage_step(stage, carry):
        @pl.when(stage < zs)
        def _():
            multiply(stage)

        @pl.when(stage > 0)
        def _():
            pass_on(stage - 1)

        @pl.when(stage == min(3, zs - 1))
        def _():
            reduce_projection()

        @pl.when(stage == zs - 1)
        def _():
            exchange()

        return carry

    lax.fori_loop(0, zs + 1, stage_step, 0)

    lane = min(128, vecs)
    for xx in range(2):
        at = slice(xx * rows, (xx + 1) * rows)
        for n in range(vecs // lane):
            re = slice(n * lane, (n + 1) * lane)
            im = slice(vecs + n * lane, vecs + (n + 1) * lane)
            both = [(ring_out[zs - 1, f, at, re].astype(F32), ring_out[zs - 1, f, at, im].astype(F32)) for f in range(half)]
            values = backward([(both[0][0], None)] + both[1:] + [(both[0][1], None)])
            for k in range(total_k):
                p_out[xx, k // kpts, k % kpts, :, re] = (values[k] * (1.0 / total_k)).astype(BF16)
    pltpu.make_async_copy(p_out.at[xh, gb], p_in.at[gb, xh], sem_p.at[1]).start()

    def send_p(i, carry):
        peer, xx = (gb + i // 2) % groups, (xh + i) % 2
        send(p_out.at[xx, peer], p_in.at[gb, xh], sem_p.at[0], sem_p.at[1], {"blk": peer, "tr": place(z, xx, c)})
        return carry

    lax.fori_loop(1, 2 * groups, send_p, 0)
    wait_bytes(p_in, sem_p.at[1])
    for k in range(kpts):
        for g in range(groups):
            value = p_in[g, 0, k].astype(F32) + p_in[g, 1, k].astype(F32)
            prhs[(k * groups + g) * rows : (k * groups + g + 1) * rows, :] = value.astype(BF16)

    own_t = count // (4 * zs)
    for m in range(zs // 2):
        at = slice(m * 8 * own_t, (m + 1) * 8 * own_t)
        value = eterm[at, :] - jnp.dot(d2[at, :], prhs[...], preferred_element_type=F32)
        for i in range(8):
            f_part[i % 2, m * 2 + i // 4, i // 2 % 2] = value[i * own_t : (i + 1) * own_t]
        pair = pl.ds(m * 2, 2)
        send(f_part.at[1 - c, pair], f_core.at[pair], sem_f_out, sem_f_in.at[m], other)
    for m in range(zs // 2):
        pair = pl.ds(m * 2, 2)
        wait_bytes(f_core.at[pair], sem_f_in.at[m])
        t_out[pair] = (f_part[c, pair] + f_core[pair]).astype(BF16)
    pltpu.make_async_copy(t_out.at[z, xh], t_in.at[z, xh], sem_t.at[1]).start()

    def send_t(i, carry):
        zz, xx = (z + i // 2) % zs, (xh + i) % 2
        send(t_out.at[zz, xx], t_in.at[z, xh], sem_t.at[0], sem_t.at[1], {"tr": place(zz, xx, c)})
        return carry

    lax.fori_loop(1, 2 * zs, send_t, 0)
    wait_bytes(t_in, sem_t.at[1])
    total = jnp.zeros(out.shape, F32)
    for zz in range(zs):
        for xx in range(2):
            total = total + t_in[zz, xx].astype(F32)
    out[...] = total

    def sent_stage(stage, carry):
        wait_bytes(s_in.at[stage, pl.ds(0, groups - 1)], sem_s_out.at[stage])
        wait_bytes(core_in.at[stage], sem_c_out.at[stage])

        @pl.when(stage < zs - 1)
        def _():
            wait_bytes(ring_out.at[stage], sem_r_out.at[stage])

        return carry

    lax.fori_loop(0, zs, sent_stage, 0)
    wait_bytes(b_in.at[pl.ds(0, groups - 1)], sem_b.at[0])
    wait_bytes(proj_in.at[pl.ds(0, groups - 1)], sem_x.at[0])
    wait_bytes(proj_in.at[pl.ds(0, groups - 1)], sem_x.at[2])
    wait_bytes(p_in.at[pl.ds(0, groups - 1)], sem_p.at[0])
    wait_bytes(p_in.at[0, 0], sem_p.at[0])
    wait_bytes(f_core, sem_f_out)
    wait_bytes(t_in.at[pl.ds(0, zs - 1)], sem_t.at[0])
    wait_bytes(t_in.at[0, 0], sem_t.at[0])


def per_device(trial, energies, kpoint_of, exchange_dens, direct_dens, coulomb, screened):
    groups, members = lax.axis_size("blk"), lax.axis_size("tr")
    member = lax.axis_index("tr")
    kpts, all_waves, waves = screened.shape
    count, vecs = trial.shape
    zs = members // 4
    rows = all_waves // groups // members
    half = groups * kpts // 2
    own_waves = exchange_dens.shape[1]
    share = own_waves // groups
    own_t = count // members
    parts = min(4, half)
    dma, vmem = pltpu.SemaphoreType.DMA, pltpu.VMEM
    scratch = [
        vmem((count, own_waves), BF16),
        vmem((count, waves), BF16),
        vmem((count, vecs), BF16),
        vmem((vecs, count), BF16),
        vmem((count, kpts * waves), BF16),
        vmem((zs, groups, 2, kpts, 2, rows, waves), BF16),
        vmem((kpts, vecs, waves), BF16),
        vmem((groups, kpts, vecs, waves), BF16),
        vmem((half, 2 * vecs, 2 * waves), BF16),
        vmem((half, 4 * rows, 2 * waves), BF16),
        vmem((zs, 2, half, 2 * rows, 2 * vecs), BF16),
        vmem((zs, half, 2 * rows, 2 * vecs), BF16),
        vmem((zs, half, 2 * rows, 2 * vecs), BF16),
        vmem((zs, half, 2 * rows, 2 * vecs), BF16),
        vmem((vecs, own_waves), BF16),
        vmem((groups, vecs, share), BF16),
        vmem((vecs, own_waves), BF16),
        vmem((count, vecs), F32),
        vmem((2, groups, kpts, rows, vecs), BF16),
        vmem((groups, 2, kpts, rows, vecs), BF16),
        vmem((kpts * groups * rows, vecs), BF16),
        vmem((2, zs, 2, own_t, vecs), F32),
        vmem((zs, 2, own_t, vecs), F32),
        vmem((zs, 2, own_t, vecs), BF16),
        vmem((zs, 2, own_t, vecs), BF16),
        dma((3,)),
        dma((zs,)),
        dma((zs,)),
        dma((2,)),
        dma((4,)),
        dma((zs,)),
        dma((zs, parts)),
        dma((zs,)),
        dma((zs, parts)),
        dma((2,)),
        dma,
        dma((zs // 2,)),
        dma((2,)),
    ]
    anywhere, in_vmem = pl.BlockSpec(memory_space=pl.ANY), pl.BlockSpec(memory_space=pltpu.VMEM)
    summed = pl.pallas_call(
        functools.partial(kernel, (groups, zs, kpts, rows, waves, vecs, parts)),
        out_shape=jax.ShapeDtypeStruct((own_t, vecs), F32),
        in_specs=[anywhere] * 4 + [in_vmem] * 2,
        out_specs=in_vmem,
        scratch_shapes=scratch,
        compiler_params=pltpu.CompilerParams(collective_id=0, has_side_effects=True, vmem_limit_bytes=48 * 1024 * 1024),
    )(
        screened.reshape(kpts, zs, 2, 2, groups, rows, waves),
        exchange_dens,
        direct_dens,
        trial,
        kpoint_of.reshape(1, count),
        coulomb.reshape(groups, share),
    )
    own_trial = lax.dynamic_slice_in_dim(trial, member * own_t, own_t, 0)
    return energies[:, None] * own_trial.astype(F32) + summed


def solution(mesh):
    in_specs = (
        P("blk", None),
        P(("blk", "tr")),
        P("blk"),
        P("blk", "tr"),
        P("blk", "tr"),
        P("tr"),
        P("blk", None, "tr"),
    )
    out_specs = P(("blk", "tr"), None)
    return jax.shard_map(
        per_device, mesh=mesh, in_specs=in_specs, out_specs=out_specs, check_vma=False
    )
```

time: 389 us -> 91.1 us (0.23); the launches traced: 383 us -> 90.8 us
  waiting for transfers between devices: 279 us -> 0 us
  Pallas kernels: 0 us -> 83.6 us
  other arithmetic: 33.9 us -> 0.7 us
  blocking collectives: 26.4 us -> 0 us
  between operations: 13.6 us -> 0.02 us
  starting transfers between devices: 10.3 us -> 0 us
  matrix products: 9.22 us -> 0 us
  local copies, waits for them, and re-layouts: 11.4 us -> 6.55 us
    reduce_scatter x3 -> x0, waiting for transfers between devices: 236 us -> none  [the longest x1 113 us: per_device(): lax.psum_scatter(2.0 * exchange_term - direct, 'tr', scatter_dimension=0,...]
    pallas_call x0 -> x1, Pallas kernels: none -> 83.6 us  [per_device(): pl.pallas_call(functools.partial(kernel, (groups, zs, kpts, rows, waves,...]
    all_to_all x2 -> x0, waiting for transfers between devices: 42.7 us -> none  [the longest x1 39 us: per_device(): s = lax.all_to_all(s, 'blk', split_axis=2, concat_axis=0, tiled=True)]
    all_gather x1 -> x0, blocking collectives: 26.4 us -> none  [per_device(): lax.all_gather((own_coulomb[:, None] * projected).astype(bf16), 'blk', ax...]
    convert_element_type x16 -> x0, other arithmetic: 21.7 us -> none  [the longest x8 16 us: per_device(): lhs.append(jnp.concatenate([a.astype(bf16), b.astype(bf16)], axis=1))]
    all_to_all x2 -> x0, starting transfers between devices: 10.1 us -> none  [the longest x1 6.08 us: per_device(): s = lax.all_to_all(s, 'blk', split_axis=2, concat_axis=0, tiled=True)]
    dot_general x5 -> x0, matrix products: 9.22 us -> none  [the longest x1 2.37 us: per_device(): jnp.dot(masked, potential.reshape(kpoints * own_waves, vectors), preferre...]
    reshape x2 -> x0, local copies, waits for them, and re-layouts: 5.93 us -> none  [the longest x1 3.48 us: per_device(): s = screened.reshape(kpoints, members, groups, rows, own_waves)]
  transfers between devices with their start and end apart: 6 -> 0, of which waited for: 5 -> 0; matrix products, arithmetic and copies ran while one was open for 9% -> 0% of each run, Pallas kernels for 0% -> 0%
where the time goes in v2:
time: 91.1 us; the launch traced here: 90.8 us
  Pallas kernels  83.6 us (92%)
  local copies, waits for them, and re-layouts  6.55 us (7%)
    pallas_call x1, Pallas kernels, per_device(): pl.pallas_call(functools.partial(kernel, (groups, zs, kpts, rows, waves,...  83.6 us
    unnamed x14, local copies, waits for them, and re-layouts  6.55 us

profile of v2, /device:TPU:1, one launch (start us, length us, event | category | flops | bytes accessed | tf_op | source)
XLA Modules:
  0.0 90.8 jit_solution(4149440843717623553)
XLA Ops:
  0.0 0.0 copy-start
  0.0 1.6 %copy-done = bf16[2,4096,128]{2,1,0:T(8,128)(2,1)S(1)} copy-done((bf16[2,4096,128]{2,1,0:T(8,128)(2,1)S(1)}, bf16[2,4096,128]{2,1,0:T(8,128)(2,1)}, u32[]{:S(2)}) %copy-start) | copy-done | bytes 2097176
  1.6 0.0 copy-start.1
  1.6 1.6 %copy-done.1 = bf16[1024,1024]{1,0:T(8,128)(2,1)S(1)} copy-done((bf16[1024,1024]{1,0:T(8,128)(2,1)S(1)}, bf16[1024,1024]{1,0:T(8,128)(2,1)}, u32[]{:S(2)}) %copy-start.1) | copy-done | bytes 2097176
  3.2 0.0 copy-start.2
  3.2 1.0 %copy-done.2 = bf16[1024,256]{1,0:T(8,128)(2,1)S(1)} copy-done((bf16[1024,256]{1,0:T(8,128)(2,1)S(1)}, bf16[1024,256]{1,0:T(8,128)(2,1)}, u32[]{:S(2)}) %copy-start.2) | copy-done | bytes 524312
  4.2 0.0 copy-start.3
  4.2 0.9 %copy-done.3 = bf16[1024,128]{1,0:T(8,128)(2,1)S(1)} copy-done((bf16[1024,128]{1,0:T(8,128)(2,1)S(1)}, bf16[1024,128]{1,0:T(8,128)(2,1)}, u32[]{:S(2)}) %copy-start.3) | copy-done | bytes 262168
  5.2 0.0 copy-start.4
  5.2 0.7 copy-done.4
  5.9 0.0 copy-start.5
  5.9 0.7 copy-done.5
  6.6 0.0 copy-start.6
  6.6 83.6 %shard_map.73 = f32[32,256]{1,0:T(8,128)S(1)} custom-call(bf16[2,8,2,2,8,16,128]{6,5,4,3,2,1,0:T(8,128)(2,1)S(1)} %bitcast.3, bf16[1024,1024]{1,0:T(8,128)(2,1)S(1)} %copy-done.1, bf16[1024,128]{1,0:T(8,128)(2,1)S(1)} %copy-done.3, bf16[1024,256]{1,0:T(8,128)(2,1)S(1)} %copy-done.2, s32[1,1024]{1,0:T(1,128)S(1)} %bitcast.4, f32[8,128]{1,0:T(8,128)S(1)} %bitcast.5), custom_call_target="tpu_custom_call" | custom-call | tf_op jit(solution)/shard_map/pallas_call | solution.py:408
  90.1 0.0 copy-done.6
  90.1 0.7 multiply_add_fusion
Async XLA Ops:
  0.0 1.6 %copy-start = (bf16[2,4096,128]{2,1,0:T(8,128)(2,1)S(1)}, bf16[2,4096,128]{2,1,0:T(8,128)(2,1)}, u32[]{:S(2)}) copy-start(bf16[2,4096,128]{2,1,0:T(8,128)(2,1)} %param.13) | copy-start | bytes 6291460
  1.6 1.6 %copy-start.1 = (bf16[1024,1024]{1,0:T(8,128)(2,1)S(1)}, bf16[1024,1024]{1,0:T(8,128)(2,1)}, u32[]{:S(2)}) copy-start(bf16[1024,1024]{1,0:T(8,128)(2,1)} %e_hbm.1) | copy-start | bytes 6291460
  3.2 1.0 %copy-start.2 = (bf16[1024,256]{1,0:T(8,128)(2,1)S(1)}, bf16[1024,256]{1,0:T(8,128)(2,1)}, u32[]{:S(2)}) copy-start(bf16[1024,256]{1,0:T(8,128)(2,1)} %t_hbm.1) | copy-start | bytes 1572868
  4.2 0.9 %copy-start.3 = (bf16[1024,128]{1,0:T(8,128)(2,1)S(1)}, bf16[1024,128]{1,0:T(8,128)(2,1)}, u32[]{:S(2)}) copy-start(bf16[1024,128]{1,0:T(8,128)(2,1)} %d_hbm.1) | copy-start | bytes 786436
  5.2 0.7 copy-start.4
  5.9 0.7 copy-start.5
  6.6 83.6 %copy-start.6 = (f32[32]{0:T(128)S(1)}, f32[32]{0:T(128)}, u32[]{:S(2)}) copy-start(f32[32]{0:T(128)} %param.8) | copy-start | bytes 388

commit v3 on v1

v3 whole, which is shorter than its diff:
```python
import functools
import math

import jax
import jax.numpy as jnp
from jax import lax
from jax.experimental import pallas as pl
from jax.experimental.pallas import tpu as pltpu
from jax.sharding import PartitionSpec as P

F32, BF16 = jnp.float32, jnp.bfloat16
WINDOW, X_AFTER = 3, 4
NT_DIMS = (((1,), (1,)), ((), ()))


def turn(value, angle):
    re, im = value
    c, s = math.cos(angle), math.sin(angle)
    if abs(s) < 1e-9:
        return value
    if abs(c) < 1e-9:
        return (None if im is None else -s * im), s * re
    if im is None:
        return c * re, s * re
    return c * re - s * im, s * re + c * im


def plus(a, b):
    return b if a is None else a if b is None else a + b


def minus(a, b):
    return a if b is None else -b if a is None else a - b


def forward(x):
    n = len(x)
    if n == 2:
        return [(x[0] + x[1], None), (x[0] - x[1], None)]
    even, odd = forward(x[0::2]), forward(x[1::2])
    out = [None] * (n // 2 + 1)
    for w in range(n // 4 + 1):
        e, o = even[w], turn(odd[w], -2 * math.pi * w / n)
        out[w] = plus(e[0], o[0]), plus(e[1], o[1])
        if w != n // 2 - w:
            re, im = minus(e[0], o[0]), minus(e[1], o[1])
            out[n // 2 - w] = re, None if im is None else -im
    return out


def backward(y):
    n = 2 * (len(y) - 1)
    if n == 2:
        return [y[0][0] + y[1][0], y[0][0] - y[1][0]]
    even, odd = [], []
    for w in range(n // 4 + 1):
        a, b = y[w], y[n // 2 - w]
        even.append((plus(a[0], b[0]), minus(a[1], b[1])))
        odd.append(turn((minus(a[0], b[0]), plus(a[1], b[1])), 2 * math.pi * w / n))
    for part in (even, odd):
        part[0], part[-1] = (part[0][0], None), (part[-1][0], None)
    out = [None] * n
    out[0::2], out[1::2] = backward(even), backward(odd)
    return out


def wait_bytes(ref, sem):
    pltpu.make_async_copy(ref, ref, sem).wait()


def send(src, dst, send_sem, recv_sem, device):
    pltpu.make_async_remote_copy(
        src_ref=src, dst_ref=dst, send_sem=send_sem, recv_sem=recv_sem,
        device_id=device, device_id_type=pl.DeviceIdType.MESH,
    ).start()


def when(condition, do):
    if isinstance(condition, bool):
        if condition:
            do()
    else:

        @pl.when(condition)
        def _():
            do()


def kernel(
    sizes, s_hbm, e_hbm, d_hbm, t_hbm, kp, coul, out,
    e, d, t, tt, d2, s_in, b_out, b_in, rhs, lhs, part, core_in, ring_out, ring_in,
    proj, proj_out, pair_in, pair_out, proj_in, scaled, eterm, p_out, p_in, prhs, f_part, f_core, t_out, t_in,
    sem_load, sem_s_out, sem_s_in, sem_b_out, sem_b_in, sem_x, sem_c_out, sem_c_in, sem_r_out, sem_r_in,
    sem_p, sem_f, sem_t,
):
    groups, zs, kpts, rows, waves, vecs, parts, pieces = sizes
    lane = vecs // pieces
    ys = groups // 2
    total_k = groups * kpts
    half = total_k // 2
    units = pieces * half
    step = units // parts
    gb = lax.axis_index("blk")
    me = lax.axis_index("tr")
    z, xh, c = me // 4, (me // 2) % 2, me % 2
    y, xl = gb // 2, gb % 2
    beside = y * 2 + 1 - xl

    def place(zz, xx, cc):
        return zz * 4 + xx * 2 + cc

    def along(j):
        return (gb + 2 * j) % groups

    other = {"tr": place(z, xh, 1 - c)}
    onward = {"tr": place((z + 1 - 2 * c + zs) % zs, xh, c)}

    loads = [pltpu.make_async_copy(a, b, sem_load.at[i]) for i, (a, b) in enumerate(((t_hbm, t), (d_hbm, d), (e_hbm, e)))]
    for load in loads:
        load.start()

    barrier = pltpu.get_barrier_semaphore()

    def greet(device):
        pl.semaphore_signal(barrier, inc=1, device_id=device, device_id_type=pl.DeviceIdType.MESH)

    greet(other)

    def greet_blk(i, carry):
        greet({"blk": (gb + i // 2) % groups, "tr": place(z, (xh + i) % 2, c)})
        return carry

    def greet_tr(i, carry):
        greet({"tr": place((z + i // 2) % zs, (xh + i) % 2, c)})
        return carry

    lax.fori_loop(1, 2 * groups, greet_blk, 0)
    lax.fori_loop(1, 2 * zs, greet_tr, 0)
    loads[0].wait()
    count = t.shape[0]
    tt[...] = t[...].T
    pl.semaphore_wait(barrier, 2 * groups + 2 * zs - 1)

    def send_s(stage, carry):
        for ab, zz in enumerate(((z - 1 - stage + 2 * zs) % zs, (z + 1 + stage) % zs)):
            pltpu.make_async_copy(s_hbm.at[:, zz, :, ab, gb], s_in.at[stage, gb, ab], sem_s_in.at[stage]).start()

        def to_peer(i, inner):
            peer = (gb + i) % groups
            for ab, zz in enumerate(((z - 1 - stage + 2 * zs) % zs, (z + 1 + stage) % zs)):
                send(s_hbm.at[:, zz, :, ab, peer], s_in.at[stage, gb, ab], sem_s_out.at[stage], sem_s_in.at[stage], {"blk": peer})
            return inner

        return lax.fori_loop(1, groups, to_peer, carry)

    send_s(0, 0)

    loads[1].wait()
    local = (kp[...] - gb * kpts).astype(F32)
    for k in range(kpts):
        mask = jnp.where(local == float(k), 1.0, 0.0).astype(BF16)
        own = jnp.dot(tt[...] * mask, d[...], preferred_element_type=F32)
        for n in range(pieces):
            b_out[n, k] = own[n * lane : (n + 1) * lane].astype(BF16)
    rest = sem_b_in.at[ys]

    def send_block(src, slot, n, recv_sem, peer):
        send(src, b_in.at[slot, n], sem_b_out, recv_sem, {"blk": peer})

    send_block(b_out.at[0], gb, 0, sem_b_in.at[0], beside)
    for j in range(1, ys):
        send_block(b_out.at[1], gb, 1, sem_b_in.at[ys - j], along(j))
    send_block(b_out.at[1], gb, 1, rest, beside)
    for j in range(1, ys):
        send_block(b_out.at[0], gb, 0, rest, along(j))
    pltpu.make_async_copy(b_out, b_in.at[gb], rest).start()

    loads[2].wait()
    own_waves = e.shape[1]
    share = own_waves // groups
    for i in range(ys):
        value = jnp.dot(tt[...], e[:, 2 * i * share : 2 * (i + 1) * share], preferred_element_type=F32)
        for j in range(2):
            proj[i, j] = value[:, j * share : (j + 1) * share]
            proj_out[i, j] = value[:, j * share : (j + 1) * share].astype(BF16)

    wait_bytes(b_in.at[0, 0], sem_b_in.at[0])
    for j in range(1, ys):
        send_block(b_in.at[beside, 0], beside, 0, rest, along(j))
    for j in range(1, ys):
        wait_bytes(b_in.at[0, 1], sem_b_in.at[j])
        send_block(b_in.at[along(j), 1], along(j), 1, rest, beside)
    lax.fori_loop(1, min(WINDOW, zs), send_s, 0)

    ring_in[0] = jnp.zeros(ring_in.shape[1:], BF16)
    unit = min(128, count)
    eye = lax.broadcasted_iota(jnp.int32, (unit, unit), 0) == lax.broadcasted_iota(jnp.int32, (unit, unit), 1)
    for i in range(count // unit):
        at = slice(i * unit, (i + 1) * unit)
        column = jnp.sum(jnp.where(eye, jnp.broadcast_to(local[:, at], (unit, unit)), 0.0), axis=1, keepdims=True)
        dens = d[at, :].astype(F32)
        for k in range(kpts):
            d2[at, k * waves : (k + 1) * waves] = (dens * jnp.where(column == float(k), 1.0, 0.0)).astype(BF16)

    wait_bytes(b_in.at[pl.ds(0, 3 * ys // 2)], rest)
    tile = min(16, lane)

    def transform_b(i, carry):
        n, row = i // (lane // tile), i % (lane // tile) * tile
        at = pl.ds(pl.multiple_of(row, tile), tile)
        low = pl.ds(pl.multiple_of(lane + row, tile), tile)
        freq = forward([b_in[q // kpts, n, q % kpts, at, :].astype(F32) for q in range(total_k)])
        zero = jnp.zeros((tile, waves), BF16)
        for f in range(half):
            re, im = (freq[0][0], freq[half][0]) if f == 0 else freq[f]
            re, im = re.astype(BF16), im.astype(BF16)
            rhs[n, f, at, 0:waves] = re
            rhs[n, f, at, waves:] = zero if f == 0 else -im
            rhs[n, f, low, 0:waves] = zero if f == 0 else im
            rhs[n, f, low, waves:] = im if f == 0 else re
        return carry

    lax.fori_loop(0, vecs // tile, transform_b, 0)

    def cut(index):
        return pl.ds(pl.multiple_of(index * share, share), share)

    def send_pair():
        send(proj_out.at[:, 1 - xl], pair_in, sem_x.at[0], sem_x.at[1], {"blk": beside})

    def add_pair():
        wait_bytes(pair_in, sem_x.at[1])
        for i in range(ys):
            pair_out[i] = (proj[i, xl] + pair_in[i].astype(F32)).astype(BF16)
        for j in range(1, ys):
            send(pair_out.at[(y + j) % ys], proj_in.at[y], sem_x.at[2], sem_x.at[3], {"blk": along(j)})

    def add_projection():
        wait_bytes(proj_in.at[pl.ds(0, ys - 1)], sem_x.at[3])
        total = proj[y, xl] + pair_in[y].astype(F32)
        for j in range(1, ys):
            total = total + proj_in[(y + j) % ys].astype(F32)
        scaled[:, cut(gb)] = (coul[pl.ds(gb, 1), :] * total).astype(BF16)
        send(scaled.at[:, cut(gb)], scaled.at[:, cut(gb)], sem_x.at[4], sem_x.at[5], {"blk": beside})
        for j in range(1, ys):
            send(scaled.at[:, cut(gb)], scaled.at[:, cut(gb)], sem_x.at[4], sem_x.at[6], {"blk": along(j)})

    def forward_scaled():
        wait_bytes(scaled.at[:, pl.ds(0, share)], sem_x.at[5])
        for j in range(1, ys):
            send(scaled.at[:, cut(beside)], scaled.at[:, cut(beside)], sem_x.at[4], sem_x.at[6], {"blk": along(j)})

    def exchange():
        wait_bytes(scaled.at[:, pl.ds(0, (groups - 2) * share)], sem_x.at[6])
        chunk_t = min(256, count)

        def do(i, carry):
            at = pl.ds(pl.multiple_of(i * chunk_t, chunk_t), chunk_t)
            eterm[at, :] = 2.0 * lax.dot_general(e[at, :], scaled[...], NT_DIMS, preferred_element_type=F32)
            return carry

        lax.fori_loop(0, count // chunk_t, do, 0)

    def transform_s(stage):
        wait_bytes(s_in.at[stage], sem_s_in.at[stage])
        when(stage + WINDOW == max(WINDOW, min(X_AFTER, zs - 1)), send_pair)
        when(stage + WINDOW < zs, lambda: send_s(stage + WINDOW, 0))
        for ab in range(2):
            for xx in range(2):
                freq = forward([s_in[stage, q // kpts, ab, q % kpts, xx].astype(F32) for q in range(total_k)])
                at = slice((ab * 2 + xx) * rows, (ab * 2 + xx + 1) * rows)
                for f in range(half):
                    re, im = (freq[0][0], freq[half][0]) if f == 0 else freq[f]
                    lhs[f, at, 0:waves] = re.astype(BF16)
                    lhs[f, at, waves:] = im.astype(BF16)

    def multiply(stage, p):
        for u in range(p * step, (p + 1) * step):
            value = lax.dot_general(lhs[u % half], rhs[u // half, u % half], NT_DIMS, preferred_element_type=F32)
            part[stage, 0, u] = value[: 2 * rows].astype(BF16)
            part[stage, 1, u] = value[2 * rows :].astype(BF16)
        at = pl.ds(p * step, step)
        send(part.at[stage, 1 - c, at], core_in.at[stage, at], sem_c_out.at[stage], sem_c_in.at[stage, p], other)

    def pass_on(stage, p):
        at = pl.ds(p * step, step)
        wait_bytes(core_in.at[stage, at], sem_c_in.at[stage, p])
        when(stage > 0, lambda: wait_bytes(ring_in.at[stage, at], sem_r_in.at[stage, p]))
        for u in range(p * step, (p + 1) * step):
            value = part[stage, c, u].astype(F32) + core_in[stage, u].astype(F32) + ring_in[stage, u].astype(F32)
            ring_out[stage, u] = value.astype(BF16)
        if not isinstance(stage, int):
            send(ring_out.at[stage, at], ring_in.at[stage + 1, at], sem_r_out.at[stage], sem_r_in.at[stage + 1, p], onward)

    transform_s(0)
    for p in range(parts):
        multiply(0, p)

    def stage_step(stage, carry):
        when(stage == min(4, zs - 1), add_pair)
        when(stage == min(6, zs - 1), add_projection)
        when(stage == min(7, zs - 1), forward_scaled)
        transform_s(stage)
        for p in range(parts):
            multiply(stage, p)
            pass_on(stage - 1, p)
        return carry

    lax.fori_loop(1, zs, stage_step, 0)

    for n in range(pieces):
        for p in range(n * parts // pieces, (n + 1) * parts // pieces):
            pass_on(zs - 1, p)
        for xx in range(2):
            at = slice(xx * rows, (xx + 1) * rows)
            both = [
                (ring_out[zs - 1, n * half + f, at, :lane].astype(F32), ring_out[zs - 1, n * half + f, at, lane:].astype(F32))
                for f in range(half)
            ]
            values = backward([(both[0][0], None)] + both[1:] + [(both[0][1], None)])
            for k in range(total_k):
                p_out[n, xx, k // kpts, k % kpts] = (values[k] * (1.0 / total_k)).astype(BF16)
        pltpu.make_async_copy(p_out.at[n, xh, gb], p_in.at[n, gb, xh], sem_p.at[1, n]).start()

        def send_p(i, carry):
            peer, xx = (gb + i // 2) % groups, (xh + i) % 2
            send(p_out.at[n, xx, peer], p_in.at[n, gb, xh], sem_p.at[0, n], sem_p.at[1, n], {"blk": peer, "tr": place(z, xx, c)})
            return carry

        lax.fori_loop(1, 2 * groups, send_p, 0)

    exchange()

    own_t = count // (4 * zs)
    for n in range(pieces):
        cols = slice(n * lane, (n + 1) * lane)
        wait_bytes(p_in.at[n], sem_p.at[1, n])
        for k in range(kpts):
            for g in range(groups):
                value = p_in[n, g, 0, k].astype(F32) + p_in[n, g, 1, k].astype(F32)
                prhs[(k * groups + g) * rows : (k * groups + g + 1) * rows, cols] = value.astype(BF16)
        for m in range(zs // 2):
            at = slice(m * 8 * own_t, (m + 1) * 8 * own_t)
            value = eterm[at, cols] - jnp.dot(d2[at, :], prhs[:, cols], preferred_element_type=F32)
            for i in range(8):
                f_part[n, i % 2, m * 2 + i // 4, i // 2 % 2] = value[i * own_t : (i + 1) * own_t]
        send(f_part.at[n, 1 - c], f_core.at[n], sem_f.at[0, n], sem_f.at[1, n], other)
    for n in range(pieces):
        wait_bytes(f_core.at[n], sem_f.at[1, n])
        t_out[n] = (f_part[n, c] + f_core[n]).astype(BF16)
        pltpu.make_async_copy(t_out.at[n, z, xh], t_in.at[n, z, xh], sem_t.at[1, n]).start()

        def send_t(i, carry):
            zz, xx = (z + i // 2) % zs, (xh + i) % 2
            send(t_out.at[n, zz, xx], t_in.at[n, z, xh], sem_t.at[0, n], sem_t.at[1, n], {"tr": place(zz, xx, c)})
            return carry

        lax.fori_loop(1, 2 * zs, send_t, 0)
    for n in range(pieces):
        wait_bytes(t_in.at[n], sem_t.at[1, n])
        total = jnp.zeros((own_t, lane), F32)
        for zz in range(zs):
            for xx in range(2):
                total = total + t_in[n, zz, xx].astype(F32)
        out[:, n * lane : (n + 1) * lane] = total

    def sent_stage(stage, carry):
        wait_bytes(s_in.at[stage, pl.ds(0, groups - 1)], sem_s_out.at[stage])
        wait_bytes(core_in.at[stage], sem_c_out.at[stage])

        @pl.when(stage < zs - 1)
        def _():
            wait_bytes(ring_out.at[stage], sem_r_out.at[stage])

        return carry

    lax.fori_loop(0, zs, sent_stage, 0)
    wait_bytes(b_in.at[pl.ds(0, groups - 1)], sem_b_out)
    wait_bytes(pair_in, sem_x.at[0])
    wait_bytes(proj_in.at[pl.ds(0, ys - 1)], sem_x.at[2])
    wait_bytes(scaled.at[:, pl.ds(0, (groups - 1) * share)], sem_x.at[4])
    for n in range(pieces):
        wait_bytes(p_in.at[n, pl.ds(0, groups - 1)], sem_p.at[0, n])
        wait_bytes(p_in.at[n, 0, 0], sem_p.at[0, n])
        wait_bytes(f_core.at[n], sem_f.at[0, n])
        wait_bytes(t_in.at[n, pl.ds(0, zs - 1)], sem_t.at[0, n])
        wait_bytes(t_in.at[n, 0, 0], sem_t.at[0, n])


def per_device(trial, energies, kpoint_of, exchange_dens, direct_dens, coulomb, screened):
    groups, members = lax.axis_size("blk"), lax.axis_size("tr")
    member = lax.axis_index("tr")
    kpts, all_waves, waves = screened.shape
    count, vecs = trial.shape
    zs = members // 4
    rows = all_waves // groups // members
    half = groups * kpts // 2
    own_waves = exchange_dens.shape[1]
    share = own_waves // groups
    own_t = count // members
    parts, pieces = 8, 2
    lane = vecs // pieces
    units = pieces * half
    ys = groups // 2
    dma, vmem = pltpu.SemaphoreType.DMA, pltpu.VMEM
    scratch = [
        vmem((count, own_waves), BF16),
        vmem((count, waves), BF16),
        vmem((count, vecs), BF16),
        vmem((vecs, count), BF16),
        vmem((count, kpts * waves), BF16),
        vmem((zs, groups, 2, kpts, 2, rows, waves), BF16),
        vmem((pieces, kpts, lane, waves), BF16),
        vmem((groups, pieces, kpts, lane, waves), BF16),
        vmem((pieces, half, 2 * lane, 2 * waves), BF16),
        vmem((half, 4 * rows, 2 * waves), BF16),
        vmem((zs, 2, units, 2 * rows, 2 * lane), BF16),
        vmem((zs, units, 2 * rows, 2 * lane), BF16),
        vmem((zs, units, 2 * rows, 2 * lane), BF16),
        vmem((zs, units, 2 * rows, 2 * lane), BF16),
        vmem((ys, 2, vecs, share), F32),
        vmem((ys, 2, vecs, share), BF16),
        vmem((ys, vecs, share), BF16),
        vmem((ys, vecs, share), BF16),
        vmem((ys, vecs, share), BF16),
        vmem((vecs, own_waves), BF16),
        vmem((count, vecs), F32),
        vmem((pieces, 2, groups, kpts, rows, lane), BF16),
        vmem((pieces, groups, 2, kpts, rows, lane), BF16),
        vmem((kpts * groups * rows, vecs), BF16),
        vmem((pieces, 2, zs, 2, own_t, lane), F32),
        vmem((pieces, zs, 2, own_t, lane), F32),
        vmem((pieces, zs, 2, own_t, lane), BF16),
        vmem((pieces, zs, 2, own_t, lane), BF16),
        dma((3,)),
        dma((zs,)),
        dma((zs,)),
        dma,
        dma((ys + 1,)),
        dma((7,)),
        dma((zs,)),
        dma((zs, parts)),
        dma((zs,)),
        dma((zs, parts)),
        dma((2, pieces)),
        dma((2, pieces)),
        dma((2, pieces)),
    ]
    anywhere, in_vmem = pl.BlockSpec(memory_space=pl.ANY), pl.BlockSpec(memory_space=pltpu.VMEM)
    summed = pl.pallas_call(
        functools.partial(kernel, (groups, zs, kpts, rows, waves, vecs, parts, pieces)),
        out_shape=jax.ShapeDtypeStruct((own_t, vecs), F32),
        in_specs=[anywhere] * 4 + [in_vmem] * 2,
        out_specs=in_vmem,
        scratch_shapes=scratch,
        compiler_params=pltpu.CompilerParams(collective_id=0, has_side_effects=True, vmem_limit_bytes=63 * 1024 * 1024),
    )(
        screened.reshape(kpts, zs, 2, 2, groups, rows, waves),
        exchange_dens,
        direct_dens,
        trial,
        kpoint_of.reshape(1, count),
        coulomb.reshape(groups, share),
    )
    own_trial = lax.dynamic_slice_in_dim(trial, member * own_t, own_t, 0)
    return energies[:, None] * own_trial.astype(F32) + summed


def solution(mesh):
    in_specs = (
        P("blk", None),
        P(("blk", "tr")),
        P("blk"),
        P("blk", "tr"),
        P("blk", "tr"),
        P("tr"),
        P("blk", None, "tr"),
    )
    out_specs = P(("blk", "tr"), None)
    return jax.shard_map(
        per_device, mesh=mesh, in_specs=in_specs, out_specs=out_specs, check_vma=False
    )
```

time: 389 us -> 79.5 us (0.20); the launches traced: 383 us -> 79.3 us
  waiting for transfers between devices: 279 us -> 0 us
  Pallas kernels: 0 us -> 77.9 us
  other arithmetic: 33.9 us -> 1.46 us
  blocking collectives: 26.4 us -> 0 us
  between operations: 13.6 us -> 0.02 us
  local copies, waits for them, and re-layouts: 11.4 us -> 0.01 us
  starting transfers between devices: 10.3 us -> 0 us
  matrix products: 9.22 us -> 0 us
    reduce_scatter x3 -> x0, waiting for transfers between devices: 236 us -> none  [the longest x1 113 us: per_device(): lax.psum_scatter(2.0 * exchange_term - direct, 'tr', scatter_dimension=0,...]
    pallas_call x0 -> x1, Pallas kernels: none -> 77.9 us  [per_device(): pl.pallas_call(functools.partial(kernel, (groups, zs, kpts, rows, waves,...]
    all_to_all x2 -> x0, waiting for transfers between devices: 42.7 us -> none  [the longest x1 39 us: per_device(): s = lax.all_to_all(s, 'blk', split_axis=2, concat_axis=0, tiled=True)]
    all_gather x1 -> x0, blocking collectives: 26.4 us -> none  [per_device(): lax.all_gather((own_coulomb[:, None] * projected).astype(bf16), 'blk', ax...]
    convert_element_type x16 -> x0, other arithmetic: 21.7 us -> none  [the longest x8 16 us: per_device(): lhs.append(jnp.concatenate([a.astype(bf16), b.astype(bf16)], axis=1))]
    all_to_all x2 -> x0, starting transfers between devices: 10.1 us -> none  [the longest x1 6.08 us: per_device(): s = lax.all_to_all(s, 'blk', split_axis=2, concat_axis=0, tiled=True)]
    dot_general x5 -> x0, matrix products: 9.22 us -> none  [the longest x1 2.37 us: per_device(): jnp.dot(masked, potential.reshape(kpoints * own_waves, vectors), preferre...]
    reshape x2 -> x0, local copies, waits for them, and re-layouts: 5.93 us -> none  [the longest x1 3.48 us: per_device(): s = screened.reshape(kpoints, members, groups, rows, own_waves)]
  transfers between devices with their start and end apart: 6 -> 0, of which waited for: 5 -> 0; matrix products, arithmetic and copies ran while one was open for 9% -> 0% of each run, Pallas kernels for 0% -> 0%
where the time goes in v3:
time: 79.5 us; the launch traced here: 79.3 us
  Pallas kernels  77.9 us (98%)
  other arithmetic  1.46 us (2%)
    pallas_call x1, Pallas kernels, per_device(): pl.pallas_call(functools.partial(kernel, (groups, zs, kpts, rows, waves,...  77.9 us

profile of v3, /device:TPU:1, one launch (start us, length us, event | category | flops | bytes accessed | tf_op | source)
XLA Modules:
  0.0 79.3 jit_solution(8453734739700000025)
XLA Ops:
  0.0 0.0 copy-start
  0.0 77.9 %shard_map.73 = f32[32,256]{1,0:T(8,128)} custom-call(bf16[2,8,2,2,8,16,128]{6,5,4,3,2,1,0:T(8,128)(2,1)} %bitcast.3, bf16[1024,1024]{1,0:T(8,128)(2,1)} %e_hbm.1, bf16[1024,128]{1,0:T(8,128)(2,1)} %d_hbm.1, bf16[1024,256]{1,0:T(8,128)(2,1)} %t_hbm.1, s32[1,1024]{1,0:T(1,128)} %bitcast.4, f32[8,128]{1,0:T(8,128)} %bitcast.5), custom_call_target="tpu_custom_call" | custom-call | tf_op jit(solution)/shard_map/pallas_call | solution.py:450
  77.9 0.0 copy-done
  77.9 1.5 %multiply_add_fusion = f32[32,256]{1,0:T(8,128)} fusion(f32[32,256]{1,0:T(8,128)} %shard_map.73, bf16[1024,256]{1,0:T(8,128)(2,1)} %t_hbm.1, s32[]{:T(128)S(6)} %select_n.3, f32[32]{0:T(128)S(1)} %copy-done), kind=kLoop, calls=%fused_computation | loop fusion | flops 24576 | bytes 82052 | tf_op jit(solution)/shard_map/add | solution.py:466
Async XLA Ops:
  0.0 77.9 %copy-start = (f32[32]{0:T(128)S(1)}, f32[32]{0:T(128)}, u32[]{:S(2)}) copy-start(f32[32]{0:T(128)} %param.8) | copy-start | bytes 388

commit v4 on v3

--- a/solution.py
+++ b/solution.py
@@ -9,7 +9,6 @@
 from jax.sharding import PartitionSpec as P
 
 F32, BF16 = jnp.float32, jnp.bfloat16
-WINDOW, X_AFTER = 3, 4
 NT_DIMS = (((1,), (1,)), ((), ()))
 
 
@@ -87,9 +86,9 @@
 
 
 def kernel(
-    sizes, s_hbm, e_hbm, d_hbm, t_hbm, kp, coul, out,
+    sizes, s_hbm, e_hbm, d_hbm, t_hbm, kp, coul, en, out,
     e, d, t, tt, d2, s_in, b_out, b_in, rhs, lhs, part, core_in, ring_out, ring_in,
-    proj, proj_out, pair_in, pair_out, proj_in, scaled, eterm, p_out, p_in, prhs, f_part, f_core, t_out, t_in,
+    proj, proj_out, proj_in, scaled, eterm, p_out, p_in, prhs, f_part, f_core, t_out, t_in,
     sem_load, sem_s_out, sem_s_in, sem_b_out, sem_b_in, sem_x, sem_c_out, sem_c_in, sem_r_out, sem_r_in,
     sem_p, sem_f, sem_t,
 ):
@@ -139,22 +138,6 @@
     loads[0].wait()
     count = t.shape[0]
     tt[...] = t[...].T
-    pl.semaphore_wait(barrier, 2 * groups + 2 * zs - 1)
-
-    def send_s(stage, carry):
-        for ab, zz in enumerate(((z - 1 - stage + 2 * zs) % zs, (z + 1 + stage) % zs)):
-            pltpu.make_async_copy(s_hbm.at[:, zz, :, ab, gb], s_in.at[stage, gb, ab], sem_s_in.at[stage]).start()
-
-        def to_peer(i, inner):
-            peer = (gb + i) % groups
-            for ab, zz in enumerate(((z - 1 - stage + 2 * zs) % zs, (z + 1 + stage) % zs)):
-                send(s_hbm.at[:, zz, :, ab, peer], s_in.at[stage, gb, ab], sem_s_out.at[stage], sem_s_in.at[stage], {"blk": peer})
-            return inner
-
-        return lax.fori_loop(1, groups, to_peer, carry)
-
-    send_s(0, 0)
-
     loads[1].wait()
     local = (kp[...] - gb * kpts).astype(F32)
     for k in range(kpts):
@@ -162,6 +145,21 @@
         own = jnp.dot(tt[...] * mask, d[...], preferred_element_type=F32)
         for n in range(pieces):
             b_out[n, k] = own[n * lane : (n + 1) * lane].astype(BF16)
+
+    pl.semaphore_wait(barrier, 2 * groups + 2 * zs - 1)
+
+    def send_s(stage, carry):
+        for ab, zz in enumerate(((z - 1 - stage + 2 * zs) % zs, (z + 1 + stage) % zs)):
+            pltpu.make_async_copy(s_hbm.at[:, zz, :, ab, gb], s_in.at[stage, gb, ab], sem_s_in.at[stage]).start()
+
+        def to_peer(i, inner):
+            peer = (gb + i) % groups
+            for ab, zz in enumerate(((z - 1 - stage + 2 * zs) % zs, (z + 1 + stage) % zs)):
+                send(s_hbm.at[:, zz, :, ab, peer], s_in.at[stage, gb, ab], sem_s_out.at[stage], sem_s_in.at[stage], {"blk": peer})
+            return inner
+
+        return lax.fori_loop(1, groups, to_peer, carry)
+
     rest = sem_b_in.at[ys]
 
     def send_block(src, slot, n, recv_sem, peer):
@@ -174,6 +172,7 @@
     for j in range(1, ys):
         send_block(b_out.at[0], gb, 0, rest, along(j))
     pltpu.make_async_copy(b_out, b_in.at[gb], rest).start()
+    send_s(0, 0)
 
     loads[2].wait()
     own_waves = e.shape[1]
@@ -190,7 +189,26 @@
     for j in range(1, ys):
         wait_bytes(b_in.at[0, 1], sem_b_in.at[j])
         send_block(b_in.at[along(j), 1], along(j), 1, rest, beside)
-    lax.fori_loop(1, min(WINDOW, zs), send_s, 0)
+
+    def cut(index):
+        return pl.ds(pl.multiple_of(index * share, share), share)
+
+    def send_projection():
+        for i in range(1, groups):
+            peer = (gb + i) % groups
+            send(proj_out.at[peer // 2, peer % 2], proj_in.at[gb], sem_x.at[0], sem_x.at[1], {"blk": peer})
+
+    def add_projection():
+        wait_bytes(proj_in.at[pl.ds(0, groups - 1)], sem_x.at[1])
+        total = proj[y, xl]
+        for i in range(1, groups):
+            total = total + proj_in[(gb + i) % groups].astype(F32)
+        scaled[:, cut(gb)] = (coul[pl.ds(gb, 1), :] * total).astype(BF16)
+        for i in range(1, groups):
+            send(scaled.at[:, cut(gb)], scaled.at[:, cut(gb)], sem_x.at[2], sem_x.at[3], {"blk": (gb + i) % groups})
+
+    lax.fori_loop(min(1, zs), min(8, zs), send_s, 0)
+    send_projection()
 
     ring_in[0] = jnp.zeros(ring_in.shape[1:], BF16)
     unit = min(128, count)
@@ -222,36 +240,8 @@
 
     lax.fori_loop(0, vecs // tile, transform_b, 0)
 
-    def cut(index):
-        return pl.ds(pl.multiple_of(index * share, share), share)
-
-    def send_pair():
-        send(proj_out.at[:, 1 - xl], pair_in, sem_x.at[0], sem_x.at[1], {"blk": beside})
-
-    def add_pair():
-        wait_bytes(pair_in, sem_x.at[1])
-        for i in range(ys):
-            pair_out[i] = (proj[i, xl] + pair_in[i].astype(F32)).astype(BF16)
-        for j in range(1, ys):
-            send(pair_out.at[(y + j) % ys], proj_in.at[y], sem_x.at[2], sem_x.at[3], {"blk": along(j)})
-
-    def add_projection():
-        wait_bytes(proj_in.at[pl.ds(0, ys - 1)], sem_x.at[3])
-        total = proj[y, xl] + pair_in[y].astype(F32)
-        for j in range(1, ys):
-            total = total + proj_in[(y + j) % ys].astype(F32)
-        scaled[:, cut(gb)] = (coul[pl.ds(gb, 1), :] * total).astype(BF16)
-        send(scaled.at[:, cut(gb)], scaled.at[:, cut(gb)], sem_x.at[4], sem_x.at[5], {"blk": beside})
-        for j in range(1, ys):
-            send(scaled.at[:, cut(gb)], scaled.at[:, cut(gb)], sem_x.at[4], sem_x.at[6], {"blk": along(j)})
-
-    def forward_scaled():
-        wait_bytes(scaled.at[:, pl.ds(0, share)], sem_x.at[5])
-        for j in range(1, ys):
-            send(scaled.at[:, cut(beside)], scaled.at[:, cut(beside)], sem_x.at[4], sem_x.at[6], {"blk": along(j)})
-
     def exchange():
-        wait_bytes(scaled.at[:, pl.ds(0, (groups - 2) * share)], sem_x.at[6])
+        wait_bytes(scaled.at[:, pl.ds(0, (groups - 1) * share)], sem_x.at[3])
         chunk_t = min(256, count)
 
         def do(i, carry):
@@ -263,8 +253,6 @@
 
     def transform_s(stage):
         wait_bytes(s_in.at[stage], sem_s_in.at[stage])
-        when(stage + WINDOW == max(WINDOW, min(X_AFTER, zs - 1)), send_pair)
-        when(stage + WINDOW < zs, lambda: send_s(stage + WINDOW, 0))
         for ab in range(2):
             for xx in range(2):
                 freq = forward([s_in[stage, q // kpts, ab, q % kpts, xx].astype(F32) for q in range(total_k)])
@@ -297,9 +285,7 @@
         multiply(0, p)
 
     def stage_step(stage, carry):
-        when(stage == min(4, zs - 1), add_pair)
-        when(stage == min(6, zs - 1), add_projection)
-        when(stage == min(7, zs - 1), forward_scaled)
+        when(stage == min(7, zs - 1), add_projection)
         transform_s(stage)
         for p in range(parts):
             multiply(stage, p)
@@ -356,9 +342,12 @@
             return carry
 
         lax.fori_loop(1, 2 * zs, send_t, 0)
+    square = lax.broadcasted_iota(jnp.int32, (own_t, own_t), 0) == lax.broadcasted_iota(jnp.int32, (own_t, own_t), 1)
+    level = jnp.sum(jnp.where(square, jnp.broadcast_to(en[...], (own_t, own_t)), 0.0), axis=1, keepdims=True)
+    mine = pl.ds(pl.multiple_of(me * own_t, own_t), own_t)
     for n in range(pieces):
+        total = level * t[mine, n * lane : (n + 1) * lane].astype(F32)
         wait_bytes(t_in.at[n], sem_t.at[1, n])
-        total = jnp.zeros((own_t, lane), F32)
         for zz in range(zs):
             for xx in range(2):
                 total = total + t_in[n, zz, xx].astype(F32)
@@ -376,9 +365,8 @@
 
     lax.fori_loop(0, zs, sent_stage, 0)
     wait_bytes(b_in.at[pl.ds(0, groups - 1)], sem_b_out)
-    wait_bytes(pair_in, sem_x.at[0])
-    wait_bytes(proj_in.at[pl.ds(0, ys - 1)], sem_x.at[2])
-    wait_bytes(scaled.at[:, pl.ds(0, (groups - 1) * share)], sem_x.at[4])
+    wait_bytes(proj_in.at[pl.ds(0, groups - 1)], sem_x.at[0])
+    wait_bytes(scaled.at[:, pl.ds(0, (groups - 1) * share)], sem_x.at[2])
     for n in range(pieces):
         wait_bytes(p_in.at[n, pl.ds(0, groups - 1)], sem_p.at[0, n])
         wait_bytes(p_in.at[n, 0, 0], sem_p.at[0, n])
@@ -389,7 +377,6 @@
 
 def per_device(trial, energies, kpoint_of, exchange_dens, direct_dens, coulomb, screened):
     groups, members = lax.axis_size("blk"), lax.axis_size("tr")
-    member = lax.axis_index("tr")
     kpts, all_waves, waves = screened.shape
     count, vecs = trial.shape
     zs = members // 4
@@ -420,9 +407,7 @@
         vmem((zs, units, 2 * rows, 2 * lane), BF16),
         vmem((ys, 2, vecs, share), F32),
         vmem((ys, 2, vecs, share), BF16),
-        vmem((ys, vecs, share), BF16),
-        vmem((ys, vecs, share), BF16),
-        vmem((ys, vecs, share), BF16),
+        vmem((groups, vecs, share), BF16),
         vmem((vecs, own_waves), BF16),
         vmem((count, vecs), F32),
         vmem((pieces, 2, groups, kpts, rows, lane), BF16),
@@ -437,7 +422,7 @@
         dma((zs,)),
         dma,
         dma((ys + 1,)),
-        dma((7,)),
+        dma((4,)),
         dma((zs,)),
         dma((zs, parts)),
         dma((zs,)),
@@ -447,10 +432,10 @@
         dma((2, pieces)),
     ]
     anywhere, in_vmem = pl.BlockSpec(memory_space=pl.ANY), pl.BlockSpec(memory_space=pltpu.VMEM)
-    summed = pl.pallas_call(
+    return pl.pallas_call(
         functools.partial(kernel, (groups, zs, kpts, rows, waves, vecs, parts, pieces)),
         out_shape=jax.ShapeDtypeStruct((own_t, vecs), F32),
-        in_specs=[anywhere] * 4 + [in_vmem] * 2,
+        in_specs=[anywhere] * 4 + [in_vmem] * 3,
         out_specs=in_vmem,
         scratch_shapes=scratch,
         compiler_params=pltpu.CompilerParams(collective_id=0, has_side_effects=True, vmem_limit_bytes=63 * 1024 * 1024),
@@ -461,9 +446,8 @@
         trial,
         kpoint_of.reshape(1, count),
         coulomb.reshape(groups, share),
+        energies.reshape(1, own_t),
     )
-    own_trial = lax.dynamic_slice_in_dim(trial, member * own_t, own_t, 0)
-    return energies[:, None] * own_trial.astype(F32) + summed
 
 
 def solution(mesh):

time: 79.5 us -> 78.3 us (0.985)
  other arithmetic: 1.46 us -> 0 us
  local copies, waits for them, and re-layouts: 0.01 us -> 1.38 us
  Pallas kernels: 77.9 us -> 76.7 us
    add x1 -> x0, other arithmetic: 1.46 us -> none  [per_device(): return energies[:, None] * own_trial.astype(F32) + summed]
    unnamed x2 -> x1, local copies, waits for them, and re-layouts: 0.01 us -> 1.38 us
    pallas_call x1, Pallas kernels: 77.9 us -> 76.7 us  [per_device(): pl.pallas_call(functools.partial(kernel, (groups, zs, kpts, rows, waves,...]
where the time goes in v4:
time: 78.3 us; the launch traced here: 78.1 us
  Pallas kernels  76.7 us (98%)
  local copies, waits for them, and re-layouts  1.38 us (2%)
    pallas_call x1, Pallas kernels, per_device(): pl.pallas_call(functools.partial(kernel, (groups, zs, kpts, rows, waves,...  76.7 us

profile of v4, /device:TPU:1, one launch (start us, length us, event | category | flops | bytes accessed | tf_op | source)
XLA Modules:
  0.0 78.1 jit_solution(9671881120122771325)
XLA Ops:
  0.0 76.7 %shard_map.73 = f32[32,256]{1,0:T(8,128)} custom-call(bf16[2,8,2,2,8,16,128]{6,5,4,3,2,1,0:T(8,128)(2,1)} %bitcast.4, bf16[1024,1024]{1,0:T(8,128)(2,1)} %e_hbm.1, bf16[1024,128]{1,0:T(8,128)(2,1)} %d_hbm.1, bf16[1024,256]{1,0:T(8,128)(2,1)} %t_hbm.1, s32[1,1024]{1,0:T(1,128)} %bitcast.5, f32[8,128]{1,0:T(8,128)} %bitcast.6, f32[1,32]{1,0:T(1,128)} %bitcast.7), custom_call_target="tpu_custom_call" | custom-call | tf_op jit(solution)/shard_map/pallas_call | solution.py:435
  76.8 1.4 %copy.9 = f32[32,256]{1,0:T(8,128)} copy(f32[32,256]{1,0:T(8,128)} %shard_map.73) | data formatting | bytes 65536

commit v5 on v4

--- a/solution.py
+++ b/solution.py
@@ -309,11 +309,12 @@
         pltpu.make_async_copy(p_out.at[n, xh, gb], p_in.at[n, gb, xh], sem_p.at[1, n]).start()
 
         def send_p(i, carry):
-            peer, xx = (gb + i // 2) % groups, (xh + i) % 2
+            peer, xx = (gb + groups // 2 + i // 2) % groups, (xh + i) % 2
             send(p_out.at[n, xx, peer], p_in.at[n, gb, xh], sem_p.at[0, n], sem_p.at[1, n], {"blk": peer, "tr": place(z, xx, c)})
             return carry
 
-        lax.fori_loop(1, 2 * groups, send_p, 0)
+        lax.fori_loop(0, groups, send_p, 0)
+        lax.fori_loop(groups + 1, 2 * groups, send_p, 0)
 
     exchange()
 
@@ -337,11 +338,12 @@
         pltpu.make_async_copy(t_out.at[n, z, xh], t_in.at[n, z, xh], sem_t.at[1, n]).start()
 
         def send_t(i, carry):
-            zz, xx = (z + i // 2) % zs, (xh + i) % 2
+            zz, xx = (z + zs // 2 + i // 2) % zs, (xh + i) % 2
             send(t_out.at[n, zz, xx], t_in.at[n, z, xh], sem_t.at[0, n], sem_t.at[1, n], {"tr": place(zz, xx, c)})
             return carry
 
-        lax.fori_loop(1, 2 * zs, send_t, 0)
+        lax.fori_loop(0, zs, send_t, 0)
+        lax.fori_loop(zs + 1, 2 * zs, send_t, 0)
     square = lax.broadcasted_iota(jnp.int32, (own_t, own_t), 0) == lax.broadcasted_iota(jnp.int32, (own_t, own_t), 1)
     level = jnp.sum(jnp.where(square, jnp.broadcast_to(en[...], (own_t, own_t)), 0.0), axis=1, keepdims=True)
     mine = pl.ds(pl.multiple_of(me * own_t, own_t), own_t)

time: 78.3 us -> 76.2 us (0.973)
  Pallas kernels: 76.7 us -> 74.6 us
    pallas_call x1, Pallas kernels: 76.7 us -> 74.6 us  [per_device(): pl.pallas_call(functools.partial(kernel, (groups, zs, kpts, rows, waves,...]
where the time goes in v5:
time: 76.2 us; the launch traced here: 76 us
  Pallas kernels  74.6 us (98%)
  local copies, waits for them, and re-layouts  1.38 us (2%)
    pallas_call x1, Pallas kernels, per_device(): pl.pallas_call(functools.partial(kernel, (groups, zs, kpts, rows, waves,...  74.6 us

profile of v5, /device:TPU:1, one launch (start us, length us, event | category | flops | bytes accessed | tf_op | source)
XLA Modules:
  0.0 76.0 jit_solution(12731940146082220375)
XLA Ops:
  0.0 74.6 %shard_map.73 = f32[32,256]{1,0:T(8,128)} custom-call(bf16[2,8,2,2,8,16,128]{6,5,4,3,2,1,0:T(8,128)(2,1)} %bitcast.4, bf16[1024,1024]{1,0:T(8,128)(2,1)} %e_hbm.1, bf16[1024,128]{1,0:T(8,128)(2,1)} %d_hbm.1, bf16[1024,256]{1,0:T(8,128)(2,1)} %t_hbm.1, s32[1,1024]{1,0:T(1,128)} %bitcast.5, f32[8,128]{1,0:T(8,128)} %bitcast.6, f32[1,32]{1,0:T(1,128)} %bitcast.7), custom_call_target="tpu_custom_call" | custom-call | tf_op jit(solution)/shard_map/pallas_call | solution.py:437
  74.6 1.4 %copy.9 = f32[32,256]{1,0:T(8,128)} copy(f32[32,256]{1,0:T(8,128)} %shard_map.73) | data formatting | bytes 65536

commit v6 on v5

--- a/solution.py
+++ b/solution.py
@@ -153,12 +153,13 @@
             pltpu.make_async_copy(s_hbm.at[:, zz, :, ab, gb], s_in.at[stage, gb, ab], sem_s_in.at[stage]).start()
 
         def to_peer(i, inner):
-            peer = (gb + i) % groups
+            peer = (gb + groups // 2 + i) % groups
             for ab, zz in enumerate(((z - 1 - stage + 2 * zs) % zs, (z + 1 + stage) % zs)):
                 send(s_hbm.at[:, zz, :, ab, peer], s_in.at[stage, gb, ab], sem_s_out.at[stage], sem_s_in.at[stage], {"blk": peer})
             return inner
 
-        return lax.fori_loop(1, groups, to_peer, carry)
+        lax.fori_loop(0, groups // 2, to_peer, 0)
+        return lax.fori_loop(groups // 2 + 1, groups, to_peer, carry)
 
     rest = sem_b_in.at[ys]
 
@@ -193,8 +194,10 @@
     def cut(index):
         return pl.ds(pl.multiple_of(index * share, share), share)
 
+    far_first = [i % groups for i in range(groups // 2, groups // 2 + groups) if i != groups]
+
     def send_projection():
-        for i in range(1, groups):
+        for i in far_first:
             peer = (gb + i) % groups
             send(proj_out.at[peer // 2, peer % 2], proj_in.at[gb], sem_x.at[0], sem_x.at[1], {"blk": peer})
 
@@ -204,7 +207,7 @@
         for i in range(1, groups):
             total = total + proj_in[(gb + i) % groups].astype(F32)
         scaled[:, cut(gb)] = (coul[pl.ds(gb, 1), :] * total).astype(BF16)
-        for i in range(1, groups):
+        for i in far_first:
             send(scaled.at[:, cut(gb)], scaled.at[:, cut(gb)], sem_x.at[2], sem_x.at[3], {"blk": (gb + i) % groups})
 
     lax.fori_loop(min(1, zs), min(8, zs), send_s, 0)

time: 76.2 us -> 77.3 us (1.014)
  Pallas kernels: 74.6 us -> 75.7 us
    pallas_call x1, Pallas kernels: 74.6 us -> 75.7 us  [per_device(): pl.pallas_call(functools.partial(kernel, (groups, zs, kpts, rows, waves,...]
where the time goes in v6:
time: 77.3 us; the launch traced here: 77.1 us
  Pallas kernels  75.7 us (98%)
  local copies, waits for them, and re-layouts  1.38 us (2%)
    pallas_call x1, Pallas kernels, per_device(): pl.pallas_call(functools.partial(kernel, (groups, zs, kpts, rows, waves,...  75.7 us

profile of v6, /device:TPU:1, one launch (start us, length us, event | category | flops | bytes accessed | tf_op | source)
XLA Modules:
  0.0 77.1 jit_solution(2402769101162334127)
XLA Ops:
  0.0 75.7 %shard_map.73 = f32[32,256]{1,0:T(8,128)} custom-call(bf16[2,8,2,2,8,16,128]{6,5,4,3,2,1,0:T(8,128)(2,1)} %bitcast.4, bf16[1024,1024]{1,0:T(8,128)(2,1)} %e_hbm.1, bf16[1024,128]{1,0:T(8,128)(2,1)} %d_hbm.1, bf16[1024,256]{1,0:T(8,128)(2,1)} %t_hbm.1, s32[1,1024]{1,0:T(1,128)} %bitcast.5, f32[8,128]{1,0:T(8,128)} %bitcast.6, f32[1,32]{1,0:T(1,128)} %bitcast.7), custom_call_target="tpu_custom_call" | custom-call | tf_op jit(solution)/shard_map/pallas_call | solution.py:440
  75.7 1.4 %copy.9 = f32[32,256]{1,0:T(8,128)} copy(f32[32,256]{1,0:T(8,128)} %shard_map.73) | data formatting | bytes 65536
